TPU v7x, 128 devices: a whole 4x4x4 slice. The times are simulated.
128 devices in a mesh: lon: 8 (over x, y_lo), sample: 16 (over y_hi, z, core).
Axes of the slice: x: 4, y: 4 (y_hi: 2, y_lo: 2; y = y_hi * 2 + y_lo), z: 4, core: 2. Of those that a mesh axis runs over, the one named last changes fastest.
Arguments:
- ocean_state: bfloat16 [16, 192, 128, 128], P('sample', None, 'lon'), may hold values from -6 to 6
- cotangent: bfloat16 [16, 192, 128, 128], P('sample', None, 'lon'), may hold values from -6 to 6
- land_sea: int32 [128, 128], P('lon'), may hold values 0 or 1
- kernel: float32 [192, 7, 7], replicated, may hold values from -0.875 to 0.875
- norm_gain: float32 [192], replicated, may hold values from 0.1 to 1.9
- in_weight: bfloat16 [192, 768], replicated, may hold values from -0.4375 to 0.4375
- out_weight: bfloat16 [768, 192], replicated, may hold values from -0.21875 to 0.21875
Outputs:
- state_out: bfloat16 [16, 192, 128, 128], P('sample', None, 'lon')
- grad_input: bfloat16 [16, 192, 128, 128], P('sample', None, 'lon')
- grad_in_weight: float32 [192, 768], P('sample')
- grad_out_weight: float32 [768, 192], P(None, 'sample')
- grad_kernel: float32 [192, 7, 7], P('sample')
- grad_gain: float32 [192], P('sample')
All inputs are finite; a program needn't handle non-finite values. No bound on the sum of `land_sea` on one device may be relied on, other than what follows from the above.
Results may differ from a plain program's by a relative error of at most 0.0056.
Values may be sent and summed in bfloat16 or wider, within the bound.
A program may use at most 128 MiB of HBM per device.

v0:
```python
import math

import jax
import jax.numpy as jnp
from jax import lax
from jax.sharding import PartitionSpec as P


def extended(array, sides, width):
    for axis, dim in sides:
        size, length = (lax.axis_size(axis), array.shape[dim])
        up = [(i, (i + 1) % size) for i in range(size)]
        down = [(j, i) for i, j in up]
        last = lax.slice_in_dim(array, length - width, length, axis=dim)
        leading = lax.slice_in_dim(array, 0, width, axis=dim)
        before = lax.ppermute(last, axis, up)
        after = lax.ppermute(leading, axis, down)
        array = jnp.concatenate([before, array, after], axis=dim)
    return array


def smooth_gate(values):
    return jax.nn.gelu(values, approximate=True)


def depthwise(padded, kernel, lon_cols, lat_rows):
    result = jnp.zeros(padded.shape[:-2] + (lon_cols, lat_rows), jnp.float32)
    for a in range(7):
        for b in range(7):
            result = result + kernel[:, a, b][:, None, None] * padded[
                ..., a : a + lon_cols, b : b + lat_rows
            ].astype(jnp.float32)
    return result


def transposed(padded, kernel, lon_cols, lat_rows):
    result = jnp.zeros(padded.shape[:-2] + (lon_cols, lat_rows), jnp.float32)
    for a in range(7):
        for b in range(7):
            result = (
                result
                + kernel[:, a, b][:, None, None]
                * padded[..., 6 - a : 6 - a + lon_cols, 6 - b : 6 - b + lat_rows]
            )
    return result


def kernel_grads(grad_conv, padded, lon_cols, lat_rows, sum_axes):
    rows_list = []
    for a in range(7):
        for b in range(7):
            rows_list.append(
                jnp.sum(
                    grad_conv * padded[..., a : a + lon_cols, b : b + lat_rows].astype(jnp.float32),
                    axis=sum_axes,
                )
            )
    return jnp.stack(rows_list, axis=1).reshape(-1, 7, 7)


def normalize(mixed_conv):
    average = jnp.mean(mixed_conv, axis=-3, keepdims=True)
    centred = mixed_conv - average
    variance = jnp.mean(centred * centred, axis=-3, keepdims=True)
    inv_scale = lax.rsqrt(variance + 1e-06)
    return (centred * inv_scale, inv_scale)


def norm_backward(grad_normed, scaled, inv_scale, norm_gain):
    grad_scaled = grad_normed * norm_gain[:, None, None]
    first = jnp.mean(grad_scaled, axis=-3, keepdims=True)
    second = jnp.mean(grad_scaled * scaled, axis=-3, keepdims=True)
    return inv_scale * (grad_scaled - first - scaled * second)


def feed_pieces(norm_block, grad_block, in_weight, out_weight):
    preact = jnp.dot(in_weight.T, norm_block, preferred_element_type=jnp.float32)
    hidden_f, pull_back = jax.vjp(smooth_gate, preact)
    hidden = hidden_f.astype(jnp.bfloat16)
    branch = jnp.dot(out_weight.T, hidden, preferred_element_type=jnp.float32)
    grad_hidden = jnp.dot(out_weight, grad_block, preferred_element_type=jnp.float32)
    grad_preact = pull_back(grad_hidden)[0].astype(jnp.bfloat16)
    out_term = jnp.dot(hidden, grad_block.T, preferred_element_type=jnp.float32)
    in_term = jnp.dot(norm_block, grad_preact.T, preferred_element_type=jnp.float32)
    grad_normed = jnp.dot(in_weight, grad_preact, preferred_element_type=jnp.float32)
    return (branch, grad_normed, in_term, out_term)


def lat_pad(field):
    return jnp.pad(field, ((0, 0), (0, 0), (0, 0), (3, 3)))


def on_device(ocean_state, cotangent, land_sea, kernel, norm_gain, in_weight, out_weight):
    samples, chans, lon_cols, lat_rows = ocean_state.shape
    hid_units = in_weight.shape[1]
    norm_factor = 1.0 / math.sqrt(
        samples * lax.axis_size("sample") * lon_cols * lax.axis_size("lon") * lat_rows
    )
    ocean_mask = land_sea.astype(jnp.float32)
    grad_branch = (cotangent.astype(jnp.float32) * ocean_mask).astype(jnp.bfloat16)
    padded = lat_pad(extended(ocean_state, (("lon", 2),), 3))
    mixed_conv = depthwise(padded, kernel, lon_cols, lat_rows)
    scaled, inv_scale = normalize(mixed_conv)
    normed = (scaled * norm_gain[:, None, None]).astype(jnp.bfloat16)
    groups = lon_cols // 8
    block_count = samples * groups

    def one_block(totals, position):
        sample_at = position // groups
        offset = position % groups * 8
        norm_block = lax.dynamic_slice(
            normed, (sample_at, 0, offset, 0), (1, chans, 8, lat_rows)
        ).reshape(chans, 8 * lat_rows)
        grad_block = lax.dynamic_slice(
            grad_branch, (sample_at, 0, offset, 0), (1, chans, 8, lat_rows)
        ).reshape(chans, 8 * lat_rows)
        branch, grad_normed, in_term, out_term = feed_pieces(
            norm_block, grad_block, in_weight, out_weight
        )
        return ((totals[0] + in_term, totals[1] + out_term), (branch, grad_normed))

    start = (jnp.zeros((chans, hid_units), jnp.float32), jnp.zeros((hid_units, chans), jnp.float32))
    weight_terms, stacked = lax.scan(one_block, start, jnp.arange(block_count, dtype=jnp.int32))

    def unblock(blocks):
        return (
            blocks.reshape(samples, groups, chans, 8, lat_rows)
            .transpose(0, 2, 1, 3, 4)
            .reshape(samples, chans, lon_cols, lat_rows)
        )

    branch = unblock(stacked[0])
    grad_normed = unblock(stacked[1])
    state_out = (ocean_mask * (ocean_state.astype(jnp.float32) + branch)).astype(jnp.bfloat16)
    gain_term = jnp.sum(grad_normed * scaled, axis=(0, 2, 3))
    grad_conv = norm_backward(grad_normed, scaled, inv_scale, norm_gain)
    grad_pad = lat_pad(extended(grad_conv, (("lon", 2),), 3))
    grad_input = (
        grad_branch.astype(jnp.float32) + transposed(grad_pad, kernel, lon_cols, lat_rows)
    ).astype(jnp.bfloat16)
    kernel_term = kernel_grads(grad_conv, padded, lon_cols, lat_rows, (0, 2, 3))
    local_terms = (weight_terms[0], weight_terms[1], kernel_term, gain_term)
    summed = lax.psum((local_terms[0], local_terms[1], local_terms[2], local_terms[3]), "lon")
    shares = (
        lax.psum_scatter(summed[0], "sample", scatter_dimension=0, tiled=True),
        lax.psum_scatter(summed[1], "sample", scatter_dimension=1, tiled=True),
        lax.psum_scatter(summed[2], "sample", scatter_dimension=0, tiled=True),
        lax.psum_scatter(summed[3], "sample", scatter_dimension=0, tiled=True),
    )
    return (
        state_out,
        grad_input,
        shares[0] * norm_factor,
        shares[1] * norm_factor,
        shares[2] * norm_factor,
        shares[3] * norm_factor,
    )


def solution(mesh):
    in_specs = (
        P("sample", None, "lon", None),
        P("sample", None, "lon", None),
        P("lon", None),
        P(),
        P(),
        P(),
        P(),
    )
    out_specs = (
        P("sample", None, "lon", None),
        P("sample", None, "lon", None),
        P("sample", None),
        P(None, "sample"),
        P("sample", None, None),
        P("sample"),
    )
    return jax.shard_map(
        on_device, mesh=mesh, in_specs=in_specs, out_specs=out_specs, check_vma=False
    )
```

profile of v0, /device:TPU:0, one launch (start us, length us, event | category | flops | bytes accessed | tf_op | source)
XLA Modules:
  0.0 353.6 jit_solution(1857222388999707267)
XLA Ops:
  7.3 1.4 copy.15
  9.6 3.9 %collective-permute-start.1 = (bf16[1,192,3,128]{3,1,2,0:T(8,128)(2,1)S(1)}, bf16[1,192,3,128]{3,1,2,0:T(8,128)(2,1)S(1)}, u32[]{:S(2)}, u32[]{:S(2)}) collective-permute-start(bf16[1,192,3,128]{3,1,2,0:T(8,128)(2,1)S(1)} %get-tuple-element.290), channel_id=1, source_target_pairs={{16,0},{32,16},{48,32},{64,48},{80,64},{96,80},{112,96},{0,112},{1... | collective-permute-start | bytes 442376 | tf_op jit(solution)/shard_map/ppermute | solution.py:17
  16.4 4.5 %collective-permute-done = bf16[1,192,3,128]{3,1,2,0:T(8,128)(2,1)S(1)} collective-permute-done((bf16[1,192,3,128]{3,1,2,0:T(8,128)(2,1)S(1)}, bf16[1,192,3,128]{3,1,2,0:T(8,128)(2,1)S(1)}, u32[]{:S(2)}, u32[]{:S(2)}) %collective-permute-start) | collective-permute-done | bytes 147488 | tf_op jit(solution)/shard_map/ppermute | solution.py:16
  21.6 1.1 select_maximum_fusion.2
  23.1 14.5 %fusion.189 = (f32[16,128]{1,0:T(8,128)S(1)}, f32[1,192,16,128]{3,1,2,0:T(8,128)S(1)}) fusion(bf16[1,192,22,134]{3,1,2,0:T(8,128)(2,1)S(1)} %select_maximum_fusion.2, f32[192]{0:T(256)S(1)} %bitcast.332, f32[192]{0:T(256)S(1)} %bitcast.334, f32[192]{0:T(256)S(1)} %bitcast.240, bf16[1,192,19,128]{3,1,2,0:T(8,128)(2,1)S(1)} %constant_dynamic-update-slice_fusion.2, ...), kind=kLoop, calls=%fused_computation.375 | loop fusion | flops 57800704 | bytes 40153856 | tf_op jit(solution)/shard_map/reduce_sum | solution.py:62
  37.8 1.5 copy-done.25
  39.3 1.7 multiply_convert_fusion
  41.0 37.2 %while.19 = (s32[]{:T(128)}, f32[192,768]{1,0:T(8,128)}, f32[768,192]{0,1:T(8,128)}, f32[2,192,1024]{2,1,0:T(8,128)}, f32[2,192,1024]{2,1,0:T(8,128)}, /*index=5...) while((s32[]{:T(128)}, f32[192,768]{1,0:T(8,128)}, ...), condition=%wide.region_3.4_spmd.clone, body=%wide.region_2.3_spmd.clone.sunk | while | flops 1842413568 | bytes 90047264 | solution.py:123
  43.5 1.2 constant_dynamic-slice_fusion.6
  46.0 3.5 fusion.232
  49.5 2.9 convolution_add_fusion.4
  52.4 3.2 convolution_add_fusion.5
  55.7 1.3 fusion.233
  58.3 1.2 copy-done.24
  62.0 1.2 constant_dynamic-slice_fusion.6
  64.5 3.5 fusion.232
  67.9 3.0 convolution_add_fusion.4
  71.0 3.4 convolution_add_fusion.5
  74.4 1.3 fusion.233
  77.1 1.2 copy-done.24
  78.2 1.7 copy.35
  80.0 1.5 copy.25
  81.8 44.4 %fusion.188 = (f32[16,768]{1,0:T(8,128)S(1)}, f32[768,16]{0,1:T(8,128)S(1)}) fusion(f32[192,768]{1,0:T(8,128)} %get-tuple-element.138, f32[768,192]{0,1:T(8,128)} %get-tuple-element.139), kind=kCustom, calls=%all-reduce-scatter.2 | all-reduce-scatter fusion | flops 393217 | bytes 1278464
  126.2 1.3 collective-permute-start.6
  127.5 1.3 collective-permute-start.5
  128.8 1.5 collective-permute-start.4
  130.3 2.5 multiply_reduce_fusion
  133.5 1.1 copy-done.6
  135.0 7.1 %fusion.178 = (f32[192]{0:T(256)S(1)}, f32[192]{0:T(256)S(1)}, f32[192]{0:T(256)S(1)}, f32[192]{0:T(256)S(1)}, f32[192]{0:T(256)S(1)}, /*index=5*/f32[192]{0:T(2...) fusion(bf16[1,192,22,134]{3,1,2,0:T(8,128)(2,1)S(1)} %select_ma, ...), kind=kLoop, calls=%fused_computation.298 | loop fusion | flops 23982720 | bytes 18921728 | tf_op jit(solution)/shard_map/reduce_sum | solution.py:53
  142.1 7.1 %fusion.177 = (f32[192]{0:T(256)S(1)}, f32[192]{0:T(256)S(1)}, f32[192]{0:T(256)S(1)}, f32[192]{0:T(256)S(1)}, f32[192]{0:T(256)S(1)}, /*index=5*/f32[192]{0:T(2...) fusion(f32[1,192,16,128]{3,1,2,0:T(8,128)S(1)} %get-tuple-eleme, ...), kind=kLoop, calls=%fused_computation.297 | loop fusion | flops 21230208 | bytes 15742464 | tf_op jit(solution)/shard_map/reduce_sum | solution.py:53
  149.3 5.1 %fusion.175 = (f32[192]{0:T(256)}, f32[192]{0:T(256)}, f32[192]{0:T(256)}, f32[192]{0:T(256)}, f32[192]{0:T(256)}, /*index=5*/f32[192]{0:T(256)}, f32[192]{0:T(2...) fusion(f32[1,192,16,128]{3,1,2,0:T(8,128)S(1)} %get-tuple-eleme, ...), kind=kLoop, calls=%fused_computation.295 | loop fusion | flops 16512576 | bytes 14173952 | tf_op jit(solution)/shard_map/reduce_sum | solution.py:53
  154.4 7.6 %collective-permute-start.7 = (f32[12,768]{1,0:T(8,128)S(1)}, f32[12,768]{1,0:T(8,128)S(1)}, u32[]{:S(2)}, u32[]{:S(2)}) collective-permute-start(f32[12,768]{1,0:T(8,128)S(1)} %slice.824), channel_id=1, source_target_pairs={{0,4},{1,5},{2,6},{3,7},{4,8},{5,9},{6,10},{7,11},{8,12},{9,13},{1... | collective-permute-start | bytes 110600
  162.0 1.8 collective-permute-start.10
  163.8 4.2 %stack.199 = f32[192,49]{0,1:T(8,128)S(1)} concatenate(f32[192,1]{0,1:T(1,128)} %bitcast.379, f32[192,1]{0,1:T(1,128)} %bitcast.380, f32[192,1]{0,1:T(1,128)} %bitcast.381, f32[192,1]{0,1:T(1,128)} %bitcast.376, f32[192,1]{0,1:T(1,128)} %bitcast.382, f32[192,1]{0,1:T(1,128)} %bitcast.383, f32[192,1]{0,1:T(1,128)} %bitcast.384, f32[192,1]{0,1:T(1,128)} %bitcast.371, ...), dimensions={1} | concatenate | bytes 75264 | tf_op jit(solution)/shard_map/stack | solution.py:58
  168.0 65.3 %all-reduce.8 = (f32[192,7,7]{0,2,1:T(8,128)S(1)}, f32[192]{0:T(256)S(1)}) all-reduce(f32[192,7,7]{0,2,1:T(8,128)S(1)} %reshape.262, f32[192]{0:T(256)S(1)} %get-tuple-element.231), channel_id=4, replica_groups=mesh['lon'=8,'sample'=16] {'sample'}, use_global_device_ids=true, to_apply=%region_60.61.clone | all-reduce | flops 9600 | bytes 76800
  234.6 1.3 collective-permute-start.9
  235.9 1.3 collective-permute-start.8
  237.2 3.3 collective-permute-start.11
  243.6 1.4 copy.26
  245.5 1.5 collective-permute-start.2
  247.0 73.9 %all-reduce.13.cloned.1.call-done = (f32[12,768]{1,0:T(8,128)}, f32[768,12]{0,1:T(8,128)}, f32[12,7,7]{0,2,1:T(8,128)}, f32[12]{0:T(128)}) async-done(((f32[12,768]{1,0:T(8,128)}, f32[768,12]{0,1:T(8,128)}, f32[12,7,7]{0,2,1:T(8,128)}, f32[12]{0:T(128)}), (f32[12,768]{1,0:T(8,128)}, f32[768,12]{0,1:T(8,128)}, f32[12,7,7]{0,2,1:T(8,128)}, f32[12]{0:T(128)})) %all-reduce.13.cloned.1.call-update) | async-done | bytes 76144 | tf_op jit(solution)/shard_map/psum | solution.py:143
  320.9 1.4 broadcast_multiply_fusion.1
  322.3 1.4 broadcast_multiply_fusion.2
  323.7 1.1 broadcast_multiply_fusion.5
  324.8 1.4 broadcast_multiply_fusion
  326.7 1.2 select_maximum_fusion
  328.2 17.2 %fusion.187 = bf16[1,192,16,128]{3,1,2,0:T(8,128)(2,1)S(1)} fusion(f32[1,192,22,134]{3,1,2,0:T(8,128)S(1)} %select_maximum_fusion, f32[1,192,16,128]{3,1,2,0:T(8,128)S(1)} %copy-done.4, f32[1,192,3,128]{3,1,2,0:T(8,128)S(1)} %collective-permute-done.2, f32[1,192,3,128]{3,1,2,0:T(8,128)S(1)} %collective-permute-done.3, ...), kind=kLoop, calls=%fused_computation.358 | loop fusion | flops 41680896 | bytes 69833472 | tf_op jit(solution)/shard_map/convert_element_type | solution.py:140
  345.4 1.4 copy.27
  (307 shorter events, 15.7 us)
Async XLA Ops:
  7.2 7.2 %copy-start.108 = (u32[128]{0:T(128)S(1)}, u32[128]{0:T(128)}, u32[]{:S(2)}) copy-start(u32[128]{0:T(128)} %constant.115) | copy-start | bytes 1540
  7.2 13.7 %copy-start.13 = (bf16[1,192,16,128]{3,2,1,0:T(8,128)(2,1)S(1)}, bf16[1,192,16,128]{3,2,1,0:T(8,128)(2,1)}, u32[]{:S(2)}) copy-start(bf16[1,192,16,128]{3,2,1,0:T(8,128)(2,1)} %param.9) | copy-start | bytes 2359300
  7.2 6.3 %copy-start.26 = (f32[192,7,7]{0,2,1:T(8,128)S(1)}, f32[192,7,7]{0,2,1:T(8,128)}, u32[]{:S(2)}) copy-start(f32[192,7,7]{0,2,1:T(8,128)} %param.12) | copy-start | bytes 112900
  7.2 7.1 %copy-start.107 = (s32[16,128]{1,0:T(8,128)S(1)}, s32[16,128]{1,0:T(8,128)}, u32[]{:S(2)}) copy-start(s32[16,128]{1,0:T(8,128)} %param.11) | copy-start | bytes 24580
  7.2 313.7 %all-reduce.13.cloned.1.call-start = ((), (), s32[]{:S(2)}) async-start(), calls=%async_computation | async-start | bytes 254976 | tf_op jit(solution)/shard_map/psum | solution.py:143
  9.6 12.0 %collective-permute-start.1 = (bf16[1,192,3,128]{3,1,2,0:T(8,128)(2,1)S(1)}, bf16[1,192,3,128]{3,1,2,0:T(8,128)(2,1)S(1)}, u32[]{:S(2)}, u32[]{:S(2)}) collective-permute-start(bf16[1,192,3,128]{3,1,2,0:T(8,128)(2,1)S(1)} %get-tuple-element.290), channel_id=1, source_target_pairs={{16,0},{32,16},{48,32},{64,48},{80,64},{96,80},{112,96},{0,112},{1... | collective-permute-start | bytes 442376 | tf_op jit(solution)/shard_map/ppermute | solution.py:17
  13.5 7.4 %collective-permute-start = (bf16[1,192,3,128]{3,1,2,0:T(8,128)(2,1)S(1)}, bf16[1,192,3,128]{3,1,2,0:T(8,128)(2,1)S(1)}, u32[]{:S(2)}, u32[]{:S(2)}) collective-permute-start(bf16[1,192,3,128]{3,1,2,0:T(8,128)(2,1)S(1)} %get-tuple-element.289), channel_id=1, source_target_pairs={{0,16},{16,32},{32,48},{48,64},{64,80},{80,96},{96,112},{112,0},{1... | collective-permute-start | bytes 442376 | tf_op jit(solution)/shard_map/ppermute | solution.py:16
  13.5 9.2 %copy-start.28 = (f32[192,1,1]{0,2,1:T(1,128)}, f32[192,1,1]{0,2,1:T(1,128)S(1)}, u32[]{:S(2)}) copy-start(f32[192,1,1]{0,2,1:T(1,128)S(1)} %get-tuple-element.300) | copy-start | bytes 2308
  13.5 9.2 %copy-start.30 = (f32[192,1,1]{0,2,1:T(1,128)}, f32[192,1,1]{0,2,1:T(1,128)S(1)}, u32[]{:S(2)}) copy-start(f32[192,1,1]{0,2,1:T(1,128)S(1)} %get-tuple-element.301) | copy-start | bytes 2308
  13.5 9.2 %copy-start.32 = (f32[192,1,1]{0,2,1:T(1,128)}, f32[192,1,1]{0,2,1:T(1,128)S(1)}, u32[]{:S(2)}) copy-start(f32[192,1,1]{0,2,1:T(1,128)S(1)} %get-tuple-element.302) | copy-start | bytes 2308
  13.6 9.2 %copy-start.34 = (f32[192,1,1]{0,2,1:T(1,128)}, f32[192,1,1]{0,2,1:T(1,128)S(1)}, u32[]{:S(2)}) copy-start(f32[192,1,1]{0,2,1:T(1,128)S(1)} %get-tuple-element.303) | copy-start | bytes 2308
  13.6 9.2 %copy-start.36 = (f32[192,1,1]{0,2,1:T(1,128)}, f32[192,1,1]{0,2,1:T(1,128)S(1)}, u32[]{:S(2)}) copy-start(f32[192,1,1]{0,2,1:T(1,128)S(1)} %get-tuple-element.304) | copy-start | bytes 2308
  13.6 9.2 %copy-start.38 = (f32[192,1,1]{0,2,1:T(1,128)}, f32[192,1,1]{0,2,1:T(1,128)S(1)}, u32[]{:S(2)}) copy-start(f32[192,1,1]{0,2,1:T(1,128)S(1)} %get-tuple-element.305) | copy-start | bytes 2308
  13.6 9.2 %copy-start.40 = (f32[192,1,1]{0,2,1:T(1,128)}, f32[192,1,1]{0,2,1:T(1,128)S(1)}, u32[]{:S(2)}) copy-start(f32[192,1,1]{0,2,1:T(1,128)S(1)} %get-tuple-element.306) | copy-start | bytes 2308
  13.6 9.2 %copy-start.42 = (f32[192,1,1]{0,2,1:T(1,128)}, f32[192,1,1]{0,2,1:T(1,128)S(1)}, u32[]{:S(2)}) copy-start(f32[192,1,1]{0,2,1:T(1,128)S(1)} %get-tuple-element.307) | copy-start | bytes 2308
  13.6 9.2 %copy-start.44 = (f32[192,1,1]{0,2,1:T(1,128)}, f32[192,1,1]{0,2,1:T(1,128)S(1)}, u32[]{:S(2)}) copy-start(f32[192,1,1]{0,2,1:T(1,128)S(1)} %get-tuple-element.308) | copy-start | bytes 2308
  13.6 9.2 %copy-start.46 = (f32[192,1,1]{0,2,1:T(1,128)}, f32[192,1,1]{0,2,1:T(1,128)S(1)}, u32[]{:S(2)}) copy-start(f32[192,1,1]{0,2,1:T(1,128)S(1)} %get-tuple-element.309) | copy-start | bytes 2308
  14.3 8.5 %copy-start.48 = (f32[192,1,1]{0,2,1:T(1,128)}, f32[192,1,1]{0,2,1:T(1,128)S(1)}, u32[]{:S(2)}) copy-start(f32[192,1,1]{0,2,1:T(1,128)S(1)} %get-tuple-element.310) | copy-start | bytes 2308
  14.3 8.5 %copy-start.50 = (f32[192,1,1]{0,2,1:T(1,128)}, f32[192,1,1]{0,2,1:T(1,128)S(1)}, u32[]{:S(2)}) copy-start(f32[192,1,1]{0,2,1:T(1,128)S(1)} %get-tuple-element.311) | copy-start | bytes 2308
  14.3 8.5 %copy-start.52 = (f32[192,1,1]{0,2,1:T(1,128)}, f32[192,1,1]{0,2,1:T(1,128)S(1)}, u32[]{:S(2)}) copy-start(f32[192,1,1]{0,2,1:T(1,128)S(1)} %get-tuple-element.312) | copy-start | bytes 2308
  16.2 5.3 %copy-start.18 = (bf16[1,192,16,128]{3,1,2,0:T(8,128)(2,1)S(1)}, bf16[1,192,16,128]{3,1,2,0:T(8,128)(2,1)}, u32[]{:S(2)}) copy-start(bf16[1,192,16,128]{3,1,2,0:T(8,128)(2,1)} %copy-done.17) | copy-start | bytes 2359300
  16.3 6.6 %copy-start.86 = (f32[192,1,1]{0,2,1:T(1,128)}, f32[192,1,1]{0,2,1:T(1,128)S(1)}, u32[]{:S(2)}) copy-start(f32[192,1,1]{0,2,1:T(1,128)S(1)} %get-tuple-element.329) | copy-start | bytes 2308
  16.3 6.6 %copy-start.88 = (f32[192,1,1]{0,2,1:T(1,128)}, f32[192,1,1]{0,2,1:T(1,128)S(1)}, u32[]{:S(2)}) copy-start(f32[192,1,1]{0,2,1:T(1,128)S(1)} %get-tuple-element.330) | copy-start | bytes 2308
  16.3 6.6 %copy-start.90 = (f32[192,1,1]{0,2,1:T(1,128)}, f32[192,1,1]{0,2,1:T(1,128)S(1)}, u32[]{:S(2)}) copy-start(f32[192,1,1]{0,2,1:T(1,128)S(1)} %get-tuple-element.331) | copy-start | bytes 2308
  16.3 6.6 %copy-start.92 = (f32[192,1,1]{0,2,1:T(1,128)}, f32[192,1,1]{0,2,1:T(1,128)S(1)}, u32[]{:S(2)}) copy-start(f32[192,1,1]{0,2,1:T(1,128)S(1)} %get-tuple-element.332) | copy-start | bytes 2308
  16.3 6.6 %copy-start.94 = (f32[192,1,1]{0,2,1:T(1,128)}, f32[192,1,1]{0,2,1:T(1,128)S(1)}, u32[]{:S(2)}) copy-start(f32[192,1,1]{0,2,1:T(1,128)S(1)} %get-tuple-element.333) | copy-start | bytes 2308
  16.3 6.6 %copy-start.96 = (f32[192,1,1]{0,2,1:T(1,128)}, f32[192,1,1]{0,2,1:T(1,128)S(1)}, u32[]{:S(2)}) copy-start(f32[192,1,1]{0,2,1:T(1,128)S(1)} %get-tuple-element.334) | copy-start | bytes 2308
  16.3 6.6 %copy-start.98 = (f32[192,1,1]{0,2,1:T(1,128)}, f32[192,1,1]{0,2,1:T(1,128)S(1)}, u32[]{:S(2)}) copy-start(f32[192,1,1]{0,2,1:T(1,128)S(1)} %get-tuple-element.335) | copy-start | bytes 2308
  16.3 6.6 %copy-start.100 = (f32[192,1,1]{0,2,1:T(1,128)}, f32[192,1,1]{0,2,1:T(1,128)S(1)}, u32[]{:S(2)}) copy-start(f32[192,1,1]{0,2,1:T(1,128)S(1)} %get-tuple-element.336) | copy-start | bytes 2308
  16.4 6.6 %copy-start.102 = (f32[192,1,1]{0,2,1:T(1,128)}, f32[192,1,1]{0,2,1:T(1,128)S(1)}, u32[]{:S(2)}) copy-start(f32[192,1,1]{0,2,1:T(1,128)S(1)} %get-tuple-element.337) | copy-start | bytes 2308
  16.4 6.6 %copy-start.104 = (f32[192,1,1]{0,2,1:T(1,128)}, f32[192,1,1]{0,2,1:T(1,128)S(1)}, u32[]{:S(2)}) copy-start(f32[192,1,1]{0,2,1:T(1,128)S(1)} %get-tuple-element.338) | copy-start | bytes 2308
  16.4 6.6 %copy-start.106 = (f32[192,1,1]{0,2,1:T(1,128)}, f32[192,1,1]{0,2,1:T(1,128)S(1)}, u32[]{:S(2)}) copy-start(f32[192,1,1]{0,2,1:T(1,128)S(1)} %get-tuple-element.339) | copy-start | bytes 2308
  64.2 3.8 %copy-start.1 = (f32[1024,768]{1,0:T(8,128)}, f32[1024,768]{1,0:T(8,128)S(1)}, u32[]{:S(2)}) copy-start(f32[1024,768]{1,0:T(8,128)S(1)} %fusion.231) | copy-start | bytes 9437188 | tf_op jit(solution)/shard_map/while
  126.2 109.7 %collective-permute-start.6 = (f32[16,768]{1,0:T(8,128)S(1)}, f32[16,768]{1,0:T(8,128)S(1)}, u32[]{:S(2)}, u32[]{:S(2)}) collective-permute-start(f32[16,768]{1,0:T(8,128)S(1)} %get-tuple-element.277), channel_id=1, source_target_pairs={{0,3},{1,4},{2,5},{3,6},{4,7},{5,8},{6,9},{7,10},{8,11},{9,12},{10... | collective-permute-start | bytes 147464
  127.5 109.7 %collective-permute-start.5 = (f32[16,768]{1,0:T(8,128)S(1)}, f32[16,768]{1,0:T(8,128)S(1)}, u32[]{:S(2)}, u32[]{:S(2)}) collective-permute-start(f32[16,768]{1,0:T(8,128)S(1)} %get-tuple-element.277), channel_id=1, source_target_pairs={{0,2},{1,3},{2,4},{3,5},{4,6},{5,7},{6,8},{7,9},{8,10},{9,11},{10,... | collective-permute-start | bytes 147464
  128.8 111.8 %collective-permute-start.4 = (f32[16,768]{1,0:T(8,128)S(1)}, f32[16,768]{1,0:T(8,128)S(1)}, u32[]{:S(2)}, u32[]{:S(2)}) collective-permute-start(f32[16,768]{1,0:T(8,128)S(1)} %get-tuple-element.277), channel_id=1, source_target_pairs={{0,1},{1,2},{2,3},{3,4},{4,5},{5,6},{6,7},{7,8},{8,9},{9,10},{10,1... | collective-permute-start | bytes 147464
  142.1 7.2 %copy-start.3 = (f32[1,192,16,128]{3,1,2,0:T(8,128)}, f32[1,192,16,128]{3,1,2,0:T(8,128)S(1)}, u32[]{:S(2)}) copy-start(f32[1,192,16,128]{3,1,2,0:T(8,128)S(1)} %get-tuple-element.279) | copy-start | bytes 4718596
  142.1 7.1 %copy-start.10 = (bf16[1,192,19,128]{3,1,2,0:T(8,128)(2,1)S(1)}, bf16[1,192,19,128]{3,1,2,0:T(8,128)(2,1)}, u32[]{:S(2)}) copy-start(bf16[1,192,19,128]{3,1,2,0:T(8,128)(2,1)} %copy-done.9) | copy-start | bytes 2801668
  142.1 7.1 %copy-start.15 = (bf16[1,192,16,128]{3,2,1,0:T(8,128)(2,1)S(1)}, bf16[1,192,16,128]{3,2,1,0:T(8,128)(2,1)}, u32[]{:S(2)}) copy-start(bf16[1,192,16,128]{3,2,1,0:T(8,128)(2,1)} %param.9) | copy-start | bytes 2359300
  154.4 89.1 %copy-start.4 = (f32[1,192,16,128]{3,1,2,0:T(8,128)S(1)}, f32[1,192,16,128]{3,1,2,0:T(8,128)}, u32[]{:S(2)}) copy-start(f32[1,192,16,128]{3,1,2,0:T(8,128)} %copy-done.3) | copy-start | bytes 4718596
  154.4 89.2 %copy-start.19 = (bf16[1,192,16,128]{3,1,2,0:T(8,128)(2,1)S(1)}, bf16[1,192,16,128]{3,1,2,0:T(8,128)(2,1)}, u32[]{:S(2)}) copy-start(bf16[1,192,16,128]{3,1,2,0:T(8,128)(2,1)} %get-tuple-element.286) | copy-start | bytes 2359300
  154.4 80.2 %collective-permute-start.7 = (f32[12,768]{1,0:T(8,128)S(1)}, f32[12,768]{1,0:T(8,128)S(1)}, u32[]{:S(2)}, u32[]{:S(2)}) collective-permute-start(f32[12,768]{1,0:T(8,128)S(1)} %slice.824), channel_id=1, source_target_pairs={{0,4},{1,5},{2,6},{3,7},{4,8},{5,9},{6,10},{7,11},{8,12},{9,13},{1... | collective-permute-start | bytes 110600
  162.0 80.3 %collective-permute-start.10 = (f32[768,16]{0,1:T(8,128)S(1)}, f32[768,16]{0,1:T(8,128)S(1)}, u32[]{:S(2)}, u32[]{:S(2)}) collective-permute-start(f32[768,16]{0,1:T(8,128)S(1)} %get-tuple-element.278), channel_id=1, source_target_pairs={{0,3},{1,4},{2,5},{3,6},{4,7},{5,8},{6,9},{7,10},{8,11},{9,12},{10... | collective-permute-start | bytes 147464
  234.6 7.7 %collective-permute-start.9 = (f32[768,16]{0,1:T(8,128)S(1)}, f32[768,16]{0,1:T(8,128)S(1)}, u32[]{:S(2)}, u32[]{:S(2)}) collective-permute-start(f32[768,16]{0,1:T(8,128)S(1)} %get-tuple-element.278), channel_id=1, source_target_pairs={{0,2},{1,3},{2,4},{3,5},{4,6},{5,7},{6,8},{7,9},{8,10},{9,11},{10,... | collective-permute-start | bytes 147464
  235.9 6.4 %collective-permute-start.8 = (f32[768,16]{0,1:T(8,128)S(1)}, f32[768,16]{0,1:T(8,128)S(1)}, u32[]{:S(2)}, u32[]{:S(2)}) collective-permute-start(f32[768,16]{0,1:T(8,128)S(1)} %get-tuple-element.278), channel_id=1, source_target_pairs={{0,1},{1,2},{2,3},{3,4},{4,5},{5,6},{6,7},{7,8},{8,9},{9,10},{10,1... | collective-permute-start | bytes 147464
  237.2 5.1 %collective-permute-start.11 = (f32[768,12]{0,1:T(8,128)S(1)}, f32[768,12]{0,1:T(8,128)S(1)}, u32[]{:S(2)}, u32[]{:S(2)}) collective-permute-start(f32[768,12]{0,1:T(8,128)S(1)} %slice.825), channel_id=1, source_target_pairs={{0,4},{1,5},{2,6},{3,7},{4,8},{5,9},{6,10},{7,11},{8,12},{9,13},{1... | collective-permute-start | bytes 110600
  245.0 81.7 %collective-permute-start.3 = (f32[1,192,3,128]{3,1,2,0:T(8,128)S(1)}, f32[1,192,3,128]{3,1,2,0:T(8,128)S(1)}, u32[]{:S(2)}, u32[]{:S(2)}) collective-permute-start(f32[1,192,3,128]{3,1,2,0:T(8,128)S(1)} %get-tuple-element.285), channel_id=1, source_target_pairs={{16,0},{32,16},{48,32},{64,48},{80,64},{96,80},{112,96},{0,112},{1... | collective-permute-start | bytes 884744 | tf_op jit(solution)/shard_map/ppermute | solution.py:17
  245.5 81.2 %collective-permute-start.2 = (f32[1,192,3,128]{3,1,2,0:T(8,128)S(1)}, f32[1,192,3,128]{3,1,2,0:T(8,128)S(1)}, u32[]{:S(2)}, u32[]{:S(2)}) collective-permute-start(f32[1,192,3,128]{3,1,2,0:T(8,128)S(1)} %get-tuple-element.284), channel_id=1, source_target_pairs={{0,16},{16,32},{32,48},{48,64},{64,80},{80,96},{96,112},{112,0},{1... | collective-permute-start | bytes 884744 | tf_op jit(solution)/shard_map/ppermute | solution.py:16
  (92 other events, 168.5 us)
Sparse Core Ops, SparseCore 0:
  243.6 77.2 all-reduce.12
where the time goes:
time: 355 us; the launch traced here: 354 us
  blocking collectives  110 us (31%)
  waiting for transfers between devices  79 us (22%)
  other arithmetic  63.3 us (18%)
  local copies, waits for them, and re-layouts  30.4 us (9%)
  starting transfers between devices  25.4 us (7%)
  matrix products  24.6 us (7%)
  between operations  17.1 us (5%)
  loops' own time  4.21 us (1%)
    unnamed x2, blocking collectives  110 us
    psum x1, waiting for transfers between devices, on_device(): lax.psum((local_terms[0], local_terms[1], local_terms[2], local_terms[3])...  73.9 us
    unnamed x8, starting transfers between devices  19.4 us
    reduce_sum x3, other arithmetic, kernel_grads(): jnp.sum(grad_conv * padded[..., a:a + lon_cols, b:b + lat_rows].astype(jn...  19.3 us
    convert_element_type x1, other arithmetic, on_device(): grad_input = (grad_branch.astype(jnp.float32) + transposed(grad_pad, kern...  17.2 us
    unnamed x213, local copies, waits for them, and re-layouts  14.8 us
    reduce_sum x1, other arithmetic, normalize(): average = jnp.mean(mixed_conv, axis=-3, keepdims=True)  14.5 us
  transfers between devices with their start and end apart: 13, of which 3 were waited for; matrix products, arithmetic and copies ran while one was open for 11% of the time, Pallas kernels for 0%

commit v1 on v0

v1 whole, which is shorter than its diff:
```python
import functools
import math

import jax
import jax.numpy as jnp
from jax import lax
from jax.experimental import pallas as pl
from jax.experimental.pallas import tpu as pltpu
from jax.sharding import PartitionSpec as P

C = 192
HID = 768
LON = 16
LAT = 128
TAPS = 7
HALO = 3
GROUP = 4
TILE = 16
OWN = 12
PACKED = 1152
BF = jnp.bfloat16
F32 = jnp.float32
MESH = pl.DeviceIdType.MESH


def tree_sum(terms):
    while len(terms) > 1:
        paired = [terms[k] + terms[k + 1] for k in range(0, len(terms) - 1, 2)]
        if len(terms) % 2:
            paired.append(terms[-1])
        terms = paired
    return terms[0]


def matmul(left, right):
    return jnp.dot(left, right, preferred_element_type=F32)


def matmul_nt(left, right):
    return lax.dot_general(left, right, (((1,), (1,)), ((), ())), preferred_element_type=F32)


def one_hot(condition):
    return jnp.where(condition, 1.0, 0.0).astype(BF)


def column(ref, at):
    return ref[pl.ds(at, C, stride=LON), :]


def kernel_body(
    n_lon,
    n_sample,
    factor,
    state_ref,
    cot_ref,
    sea_ref,
    taps_ref,
    gain_ref,
    win_ref,
    wout_ref,
    sout_ref,
    gin_ref,
    gwin_ref,
    gwout_ref,
    gk_ref,
    gg_ref,
    x32,
    c32,
    xa,
    ga,
    xf,
    kb,
    kf,
    flat_taps,
    spread_to,
    mixed_buf,
    gainb,
    win_t,
    wout_t,
    shift_b,
    shift_g,
    pick,
    ybuf,
    gshift,
    prod,
    hid_buf,
    gp_buf,
    acc_in,
    acc_out,
    acc_gain,
    dks,
    stage,
    wsend,
    wcore,
    wmid,
    wparts,
    wslab,
    ksend,
    kcore,
    kmid,
    kparts,
    kslab,
    send,
    recv,
):
    remote = n_lon > 1
    if remote:
        lon = lax.axis_index("lon")
        sample = lax.axis_index("sample")
        core = lax.rem(sample, 2)
        owner = sample // 2
        n_own = n_sample // 2
        partner = {"sample": sample + 1 - 2 * core}
        right = {"lon": lax.rem(lon + 1, n_lon)}
        left = {"lon": lax.rem(lon + n_lon - 1, n_lon)}
        owners = [lax.rem(owner + d, n_own) for d in range(1, n_own)]
        slabs = [lax.rem(lon + d, n_lon) for d in range(1, n_lon)]
        peers = (
            [partner]
            + [{"sample": 2 * other + core} for other in owners]
            + [{"lon": other} for other in slabs]
        )
        barrier = pltpu.get_barrier_semaphore()
        for peer in peers:
            pl.semaphore_signal(barrier, inc=1, device_id=peer, device_id_type=MESH)

        def copy(src, dst, slot, peer):
            return pltpu.make_async_remote_copy(
                src_ref=src,
                dst_ref=dst,
                send_sem=send.at[slot],
                recv_sem=recv.at[slot],
                device_id=peer,
                device_id_type=MESH,
            )

    def halo_copies(ref, slot):
        return (
            copy(ref.at[pl.ds(LON, HALO)], ref.at[pl.ds(0, HALO)], slot, right),
            copy(ref.at[pl.ds(HALO, HALO)], ref.at[pl.ds(LON + HALO, HALO)], slot + 1, left),
        )

    def local_halo(ref):
        ref[0:HALO] = ref[LON : LON + HALO]
        ref[LON + HALO : LON + 2 * HALO] = ref[HALO : 2 * HALO]

    x32[...] = state_ref[...].astype(F32).reshape(C * LON, LAT)
    for i in (13, 14, 15, 0, 1, 2):
        own = column(x32, i)
        xf[HALO + i] = own
        xa[HALO + i] = own.astype(BF)
    if remote:
        pl.semaphore_wait(barrier, len(peers))
        x_halo = halo_copies(xa, 0)
        for one in x_halo:
            one.start()
    for i in range(3, 13):
        own = column(x32, i)
        xf[HALO + i] = own
        xa[HALO + i] = own.astype(BF)
    c32[...] = cot_ref[...].astype(F32).reshape(C * LON, LAT)

    taps = TAPS * TAPS
    flat_taps[...] = jnp.zeros_like(flat_taps)
    for a in range(TAPS):
        flat_taps[:, 8 * a : 8 * a + TAPS] = taps_ref[:, a, :]
    rest = flat_taps[...]
    pieces = []
    for _ in range(3):
        piece = rest.astype(BF)
        pieces.append(piece)
        rest = rest - piece.astype(F32)
    split = jnp.concatenate(pieces, axis=1)
    place = lax.broadcasted_iota(jnp.int32, (3 * LAT, LAT), 0) % LAT
    for a in range(TAPS):
        for b in range(TAPS):
            t = a * TAPS + b
            spread_to[:, t * LAT : (t + 1) * LAT] = one_hot(place == 8 * a + b)
    kf[...] = matmul(split, spread_to[...])
    for t in range(taps):
        kb[t] = kf[:, t * LAT : (t + 1) * LAT].astype(BF)
    gainb[...] = jnp.broadcast_to(gain_ref[...], (LAT, C)).T
    win_t[...] = win_ref[...].T
    wout_t[...] = wout_ref[...].T
    rows = lax.broadcasted_iota(jnp.int32, (LAT, LAT), 0)
    lanes = lax.broadcasted_iota(jnp.int32, (LAT, LAT), 1)
    for b in range(TAPS):
        backward = one_hot(rows == lanes - (b - HALO))
        shift_b[b * LAT : (b + 1) * LAT, :] = backward
        shift_g[:, b * LAT : (b + 1) * LAT] = backward
    for t in range(TAPS * TAPS + 1):
        pick[t * LAT : (t + 1) * LAT, :] = one_hot(lanes == t)

    acc_in[...] = jnp.zeros_like(acc_in)
    acc_out[...] = jnp.zeros_like(acc_out)
    acc_gain[...] = jnp.zeros_like(acc_gain)

    def filtered(field, col, flip, shifts):
        def one_tile(tile, carry):
            at = pl.multiple_of(tile * TILE, TILE)
            window = field[pl.ds(col, GROUP + 2 * HALO), pl.ds(at, TILE), :]
            for b in range(TAPS):
                terms = []
                for a in range(TAPS):
                    first = 2 * HALO - a if flip else a
                    weight = kb[a * TAPS + b, pl.ds(at, TILE), :]
                    terms.append(weight[None] * window[first : first + GROUP])
                ybuf[:, pl.ds(at, TILE), b * LAT : (b + 1) * LAT] = tree_sum(terms)
            return carry

        lax.fori_loop(0, C // TILE, one_tile, 0)
        flat = ybuf[...].reshape(GROUP * C, TAPS * LAT)
        return matmul(flat, shifts[...]).reshape(GROUP, C, LAT)

    def filtered_exact(col):
        lane = lax.broadcasted_iota(jnp.int32, (GROUP, 8, LAT), 2)

        def one_tile(tile, carry):
            at = pl.multiple_of(tile * 8, 8)
            window = xf[pl.ds(col, GROUP + 2 * HALO), pl.ds(at, 8), :]
            total = None
            for b in range(TAPS):
                terms = [
                    kf[pl.ds(at, 8), (a * TAPS + b) * LAT : (a * TAPS + b + 1) * LAT][None]
                    * window[a : a + GROUP]
                    for a in range(TAPS)
                ]
                part = tree_sum(terms)
                by = b - HALO
                if by != 0:
                    turned = pltpu.roll(part, (-by) % LAT, axis=2)
                    inside = lane < LAT - by if by > 0 else lane >= -by
                    part = jnp.where(inside, turned, 0.0)
                total = part if total is None else total + part
            mixed_buf[:, pl.ds(at, 8), :] = total
            return carry

        lax.fori_loop(0, C // 8, one_tile, 0)
        return mixed_buf[...]

    def masks(col):
        return [sea_ref[pl.ds(col + k, 1), :].astype(F32) for k in range(GROUP)]

    def side_by_side(parts):
        return jnp.concatenate([parts[k] for k in range(GROUP)], axis=1)

    def forward_group(col):
        mixed = filtered_exact(col)
        centred = mixed - jnp.mean(mixed, axis=1, keepdims=True)
        variance = jnp.mean(centred * centred, axis=1, keepdims=True)
        inv_scale = lax.rsqrt(variance + 1e-06)
        scaled = centred * inv_scale
        gain = gainb[...]
        normed = side_by_side((scaled * gain[None]).astype(BF))
        mask = masks(col)
        grad_out = side_by_side([(column(c32, col + k) * mask[k]).astype(BF) for k in range(GROUP)])
        block = 128
        for h in range(0, HID, block):
            pre = matmul(win_t[h : h + block, :], normed)
            grad_hidden = matmul(wout_ref[h : h + block, :], grad_out)
            square = pre * pre
            inner = pre * (0.7978845608028654 + 0.035677408136300125 * square)
            gate = 0.5 + 0.5 * jnp.tanh(inner)
            hidden = pre * gate
            slope = gate + hidden * (1.0 - gate) * (
                1.5957691216057308 + 0.21406444881780074 * square
            )
            hid_buf[h : h + block, :] = hidden.astype(BF)
            gp_buf[h : h + block, :] = (grad_hidden * slope).astype(BF)
        branch = matmul(wout_t[...], hid_buf[...])
        grad_normed = matmul(win_ref[...], gp_buf[...])
        acc_out[...] += matmul_nt(grad_out, hid_buf[...])
        acc_in[...] += matmul_nt(normed, gp_buf[...])
        for k in range(GROUP):
            lane = slice(k * LAT, (k + 1) * LAT)
            at = pl.ds(col + k, C, stride=LON)
            x32[at, :] = mask[k] * (x32[at, :] + branch[:, lane])
            grad = grad_normed[:, lane]
            product = grad * scaled[k]
            acc_gain[...] += product
            grad_scaled = grad * gain
            first = jnp.mean(grad_scaled, axis=0, keepdims=True)
            second = jnp.mean(product * gain, axis=0, keepdims=True)
            grad_conv = inv_scale[k] * (grad_scaled - first - scaled[k] * second)
            ga[HALO + col + k] = grad_conv.astype(BF)

    def fill_halo():
        for i in (0, 1, 2, 19, 20, 21):
            xf[i] = xa[i].astype(F32)

    def one_group(step, carry):
        if remote:

            @pl.when(step == 2)
            def _():
                for one in x_halo:
                    one.wait()
                fill_halo()

        forward_group(lax.rem(GROUP + step * GROUP, LON))
        return carry

    if not remote:
        local_halo(xa)
        fill_halo()
    lax.fori_loop(0, LON // GROUP, one_group, 0)

    if remote:
        g_halo = halo_copies(ga, 2)
        for one in g_halo:
            one.start()
    else:
        local_halo(ga)

    for o in range(16):
        at = OWN * o
        wide = HID // 2
        stage[o, 0:12, 0:HID] = acc_in[at : at + 12, :]
        stage[o, 12:16, 0:HID] = acc_out[at : at + 4, :]
        stage[o, 0:8, HID:PACKED] = acc_out[at + 4 : at + 12, 0:wide]
        stage[o, 8:16, HID:PACKED] = acc_out[at + 4 : at + 12, wide:HID]
    for o in range(16):
        wsend[o % 2, o // 2] = stage[o].astype(BF)

    def reduction(base, packed, from_core, middle, parts, slab, kind):
        def core_copy():
            return copy(packed.at[1 - core], from_core, base, partner)

        def owner_copies():
            return [
                copy(middle.at[other], parts.at[d], base + 1 + d, {"sample": 2 * other + core})
                for d, other in enumerate(owners)
            ]

        def slab_copies():
            return [
                copy(slab.at[lon], slab.at[lon], base + 1 + len(owners) + d, {"lon": other})
                for d, other in enumerate(slabs)
            ]

        def start_core():
            core_copy().start()

        def start_owners():
            core_copy().wait()
            middle[...] = (packed[core].astype(F32) + from_core[...].astype(F32)).astype(kind)
            for one in owner_copies():
                one.start()

        def start_slabs():
            for one in owner_copies():
                one.wait()
            total = middle[owner].astype(F32)
            for d in range(len(owners)):
                total = total + parts[d].astype(F32)
            slab[lon] = total.astype(kind)
            for one in slab_copies():
                one.start()

        def finish():
            for one in slab_copies():
                one.wait()
            total = slab[0].astype(F32)
            for other in range(1, n_lon):
                total = total + slab[other].astype(F32)
            return total * factor

        return start_core, start_owners, start_slabs, finish

    if remote:
        w_core, w_owners, w_slabs, w_finish = reduction(
            4, wsend, wcore, wmid, wparts, wslab, BF
        )
        k_core, k_owners, k_slabs, k_finish = reduction(
            19, ksend, kcore, kmid, kparts, kslab, F32
        )
        w_core()

    def shifted(i, carry):
        gshift[i] = matmul(ga[HALO + i], shift_g[...]).astype(BF)
        return carry

    lax.fori_loop(0, LON, shifted, 0)
    if remote:
        w_owners()

    def products(tile, carry):
        at = pl.multiple_of(tile * TILE, TILE)
        for b in range(TAPS):
            grads = gshift[:, pl.ds(at, TILE), b * LAT : (b + 1) * LAT]
            for a in range(TAPS):
                field = xa[a : a + LON, pl.ds(at, TILE), :]
                terms = grads * field
                t = a * TAPS + b
                prod[pl.ds(at, TILE), t * LAT : (t + 1) * LAT] = tree_sum(
                    [terms[k] for k in range(LON)]
                )
        return carry

    lax.fori_loop(0, C // TILE, products, 0)
    prod[:, TAPS * TAPS * LAT :] = acc_gain[...].astype(BF)
    dks[0:C, :] = matmul(prod[...], pick[...])
    dks[C : C + 16, :] = jnp.zeros((16, LAT), F32)
    for o in range(16):
        ksend[o % 2, o // 2] = dks[OWN * o : OWN * o + 16, :]
    if remote:
        k_core()

    def backward_group(col):
        spread = filtered(ga, col, True, shift_b)
        mask = masks(col)
        for k in range(GROUP):
            at = pl.ds(col + k, C, stride=LON)
            c32[at, :] = c32[at, :] * mask[k] + spread[k]

    def one_back(step, carry):
        backward_group(lax.rem(GROUP + step * GROUP, LON))
        return carry

    if remote:
        w_slabs()
    lax.fori_loop(0, 2, one_back, 0)
    if remote:
        k_owners()
        for one in g_halo:
            one.wait()
    lax.fori_loop(2, 4, one_back, 0)
    if remote:
        k_slabs()
    sout_ref[...] = x32[...].reshape(C, LON, LAT).astype(BF)
    gin_ref[...] = c32[...].reshape(C, LON, LAT).astype(BF)
    if remote:
        weights = w_finish()
        small = k_finish()
    else:
        weights = wsend[0, 0].astype(F32) * factor
        small = ksend[0, 0] * factor
    wide = HID // 2
    gwin_ref[...] = weights[0:12, 0:HID]
    stage[0, 0:4, 0:HID] = weights[12:16, 0:HID]
    stage[0, 4:12, 0:wide] = weights[0:8, HID:PACKED]
    stage[0, 4:12, wide:HID] = weights[8:16, HID:PACKED]
    gwout_ref[...] = stage[0, :, 0:HID].T[:, 0:OWN]
    for a in range(TAPS):
        gk_ref[:, a, :] = small[0:OWN, a * TAPS : (a + 1) * TAPS]
    gg_ref[...] = small.T[TAPS * TAPS : TAPS * TAPS + 1, 0:OWN]


def block(n_lon, n_sample, factor, state, cot, sea, taps, gain, win, wout):
    vmem = pl.BlockSpec(memory_space=pltpu.VMEM)
    shape = jax.ShapeDtypeStruct
    outs = (
        shape((C, LON, LAT), BF),
        shape((C, LON, LAT), BF),
        shape((OWN, HID), F32),
        shape((HID, OWN), F32),
        shape((OWN, TAPS, TAPS), F32),
        shape((1, OWN), F32),
    )
    scratch = [
        pltpu.VMEM((C * LON, LAT), F32),
        pltpu.VMEM((C * LON, LAT), F32),
        pltpu.VMEM((LON + 2 * HALO, C, LAT), BF),
        pltpu.VMEM((LON + 2 * HALO, C, LAT), BF),
        pltpu.VMEM((LON + 2 * HALO, C, LAT), F32),
        pltpu.VMEM((TAPS * TAPS, C, LAT), BF),
        pltpu.VMEM((C, TAPS * TAPS * LAT), F32),
        pltpu.VMEM((C, LAT), F32),
        pltpu.VMEM((3 * LAT, TAPS * TAPS * LAT), BF),
        pltpu.VMEM((GROUP, C, LAT), F32),
        pltpu.VMEM((C, LAT), F32),
        pltpu.VMEM((HID, C), BF),
        pltpu.VMEM((C, HID), BF),
        pltpu.VMEM((TAPS * LAT, LAT), BF),
        pltpu.VMEM((LAT, TAPS * LAT), BF),
        pltpu.VMEM(((TAPS * TAPS + 1) * LAT, LAT), BF),
        pltpu.VMEM((GROUP, C, TAPS * LAT), BF),
        pltpu.VMEM((LON, C, TAPS * LAT), BF),
        pltpu.VMEM((C, (TAPS * TAPS + 1) * LAT), BF),
        pltpu.VMEM((HID, GROUP * LAT), BF),
        pltpu.VMEM((HID, GROUP * LAT), BF),
        pltpu.VMEM((C, HID), F32),
        pltpu.VMEM((C, HID), F32),
        pltpu.VMEM((C, LAT), F32),
        pltpu.VMEM((C + 16, LAT), F32),
        pltpu.VMEM((16, 16, PACKED), F32),
        pltpu.VMEM((2, 8, 16, PACKED), BF),
        pltpu.VMEM((8, 16, PACKED), BF),
        pltpu.VMEM((8, 16, PACKED), BF),
        pltpu.VMEM((7, 16, PACKED), BF),
        pltpu.VMEM((8, 16, PACKED), BF),
        pltpu.VMEM((2, 8, 16, LAT), F32),
        pltpu.VMEM((8, 16, LAT), F32),
        pltpu.VMEM((8, 16, LAT), F32),
        pltpu.VMEM((7, 16, LAT), F32),
        pltpu.VMEM((8, 16, LAT), F32),
        pltpu.SemaphoreType.DMA((34,)),
        pltpu.SemaphoreType.DMA((34,)),
    ]
    extra = dict(collective_id=0, has_side_effects=True) if n_lon > 1 else {}
    return pl.pallas_call(
        functools.partial(kernel_body, n_lon, n_sample, factor),
        out_shape=outs,
        in_specs=[vmem] * 7,
        out_specs=(vmem,) * 6,
        scratch_shapes=scratch,
        compiler_params=pltpu.CompilerParams(vmem_limit_bytes=60 * 1024 * 1024, **extra),
    )(
        state.reshape(C, LON, LAT),
        cot.reshape(C, LON, LAT),
        sea,
        taps,
        gain.reshape(1, C),
        win,
        wout,
    )


def solution(mesh):
    n_lon, n_sample = mesh.shape["lon"], mesh.shape["sample"]
    factor = 1.0 / math.sqrt(n_sample * n_lon * LON * LAT)

    def on_device(state, cot, sea, taps, gain, win, wout):
        out = block(n_lon, n_sample, factor, state, cot, sea, taps, gain, win, wout)
        shape = state.shape
        return (
            out[0].reshape(shape),
            out[1].reshape(shape),
            out[2],
            out[3],
            out[4],
            out[5].reshape(OWN),
        )

    slab = P("sample", None, "lon", None)
    return jax.shard_map(
        on_device,
        mesh=mesh,
        in_specs=(slab, slab, P("lon", None), P(), P(), P(), P()),
        out_specs=(
            slab,
            slab,
            P("sample", None),
            P(None, "sample"),
            P("sample", None, None),
            P("sample"),
        ),
        check_vma=False,
    )
```

time: 355 us -> 72.3 us (0.20)
  blocking collectives: 110 us -> 0 us
  waiting for transfers between devices: 79 us -> 0 us
  other arithmetic: 63.3 us -> 0 us
  Pallas kernels: 0 us -> 60.7 us
  starting transfers between devices: 25.4 us -> 0 us
  matrix products: 24.6 us -> 0 us
  local copies, waits for them, and re-layouts: 30.4 us -> 10.6 us
  between operations: 17.1 us -> 0.66 us
  loops' own time: 4.21 us -> 0 us
    unnamed x2 -> x0, blocking collectives: 110 us -> none
    psum x1 -> x0, waiting for transfers between devices: 73.9 us -> none  [on_device(): lax.psum((local_terms[0], local_terms[1], local_terms[2], local_terms[3])...]
    pallas_call x0 -> x1, Pallas kernels: none -> 60.7 us  [block(): pl.pallas_call(functools.partial(kernel_body, n_lon, n_sample, factor), o...]
    reduce_sum x7 -> x0, other arithmetic: 36.8 us -> none  [the longest x3 19.3 us: kernel_grads(): jnp.sum(grad_conv * padded[..., a:a + lon_cols, b:b + lat_rows].astype(jn...]
    dot_general x12 -> x0, matrix products: 24.6 us -> none  [the longest x2 6.92 us: feed_pieces(): jnp.dot(out_weight, grad_block, preferred_element_type=jnp.float32)]
    unnamed x8 -> x0, starting transfers between devices: 19.4 us -> none
    convert_element_type x3 -> x0, other arithmetic: 18.8 us -> none  [the longest x1 17.2 us: on_device(): grad_input = (grad_branch.astype(jnp.float32) + transposed(grad_pad, kern...]
    ppermute x4 -> x0, starting transfers between devices: 5.95 us -> none  [the longest x2 4.4 us: extended(): after = lax.ppermute(leading, axis, down)]
  transfers between devices with their start and end apart: 13 -> 0, of which waited for: 3 -> 0; matrix products, arithmetic and copies ran while one was open for 11% -> 0% of each run, Pallas kernels for 0% -> 0%
where the time goes in v1:
time: 72.3 us; the launch traced here: 72 us
  Pallas kernels  60.7 us (84%)
  local copies, waits for them, and re-layouts  10.6 us (15%)
    pallas_call x1, Pallas kernels, block(): pl.pallas_call(functools.partial(kernel_body, n_lon, n_sample, factor), o...  60.7 us
    unnamed x16, local copies, waits for them, and re-layouts  10.6 us

profile of v1, /device:TPU:0, one launch (start us, length us, event | category | flops | bytes accessed | tf_op | source)
XLA Modules:
  0.0 72.0 jit_solution(781726725004489273)
XLA Ops:
  0.6 0.0 copy-start.1
  0.6 1.9 %copy.14.wout_ref = bf16[768,192]{1,0:T(8,128)(2,1)} copy(bf16[768,192]{0,1:T(8,128)(2,1)} %param.13) | data formatting | bytes 589824 | tf_op args[6]
  2.5 0.0 copy-done.1
  2.5 1.2 %copy.13.taps_ref = f32[192,7,7]{2,1,0:T(8,128)} copy(f32[192,7,7]{0,2,1:T(8,128)S(1)} %copy-done.1) | data formatting | bytes 75264 | tf_op args[3]
  3.7 60.7 %shard_map.118 = (bf16[192,16,128]{2,1,0:T(8,128)(2,1)}, bf16[192,16,128]{2,1,0:T(8,128)(2,1)}, f32[12,768]{1,0:T(8,128)}, f32[768,12]{1,0:T(8,128)}, f32[12,7,7]{2,1,0:T(8,128)}, /*index=5*/f32[1,12]{1,0:T(1,128)}) custom-call(bf16[192,16,128]{2,1,0:T(8,128)(2,1)} %bitcast.8, bf16[192,16,128]{2,1,0:T(8,128)(2,1)} %bitcast.9, s32[16,128]{1,0:T(8,128)} %sea_ref.1, ...), custom_call_target="tpu_custom_call" | custom-call | tf_op jit(solution)/shard_map/pallas_call | solution.py:502
  64.5 1.5 %copy.16 = f32[12,7,7]{0,2,1:T(8,128)} copy(f32[12,7,7]{2,1,0:T(8,128)} %get-tuple-element.22) | data formatting | bytes 4704
  66.0 1.8 %copy.15 = f32[768,12]{0,1:T(8,128)} copy(f32[768,12]{1,0:T(8,128)} %get-tuple-element.21) | data formatting | bytes 73728
  67.8 0.0 copy-start
  67.8 2.2 %copy.21 = bf16[1,192,16,128]{3,2,1,0:T(8,128)(2,1)} copy(bf16[1,192,16,128]{3,2,1,0:T(8,128)(2,1)} %bitcast.7) | data formatting | bytes 1572864
  70.0 0.0 copy-done
  70.0 0.0 copy-start.2
  70.0 0.9 %copy.22 = bf16[1,192,16,128]{3,2,1,0:T(8,128)(2,1)} copy(bf16[1,192,16,128]{3,2,1,0:T(8,128)(2,1)S(1)} %bitcast.6) | data formatting | bytes 1572864
  70.9 0.0 copy-done.2
  70.9 0.0 copy-start.3
  70.9 0.6 copy.23
  71.5 0.0 copy-done.3
  71.5 0.5 copy.24
Async XLA Ops:
  0.6 1.9 %copy-start.1 = (f32[192,7,7]{0,2,1:T(8,128)S(1)}, f32[192,7,7]{0,2,1:T(8,128)}, u32[]{:S(2)}) copy-start(f32[192,7,7]{0,2,1:T(8,128)} %param.10) | copy-start | bytes 112900
  67.8 2.2 %copy-start = (bf16[192,16,128]{2,1,0:T(8,128)(2,1)S(1)}, bf16[192,16,128]{2,1,0:T(8,128)(2,1)}, u32[]{:S(2)}) copy-start(bf16[192,16,128]{2,1,0:T(8,128)(2,1)} %get-tuple-element.13) | copy-start | bytes 2359300
  70.0 0.9 %copy-start.2 = (f32[12,768]{1,0:T(8,128)S(1)}, f32[12,768]{1,0:T(8,128)}, u32[]{:S(2)}) copy-start(f32[12,768]{1,0:T(8,128)} %get-tuple-element.32) | copy-start | bytes 110596
  70.9 0.6 copy-start.3

commit v2 on v1

--- a/solution.py
+++ b/solution.py
@@ -3,6 +3,7 @@
 
 import jax
 import jax.numpy as jnp
+import numpy as np
 from jax import lax
 from jax.experimental import pallas as pl
 from jax.experimental.pallas import tpu as pltpu
@@ -12,6 +13,8 @@
 HID = 768
 LON = 16
 LAT = 128
+PERIOD = 131
+SPEC = 256
 TAPS = 7
 HALO = 3
 GROUP = 4
@@ -40,8 +43,56 @@
     return lax.dot_general(left, right, (((1,), (1,)), ((), ())), preferred_element_type=F32)
 
 
-def one_hot(condition):
-    return jnp.where(condition, 1.0, 0.0).astype(BF)
+def split_constant(values):
+    high = values.astype(BF)
+    low = (values - high.astype(np.float64)).astype(BF)
+    return high, low
+
+
+def spectral_constants():
+    angle = 2.0 * math.pi / PERIOD
+    row = np.arange(LAT)
+    field_f, field_b = np.zeros((LAT, SPEC)), np.zeros((LAT, SPEC))
+    back_f, back_b = np.zeros((SPEC, LAT)), np.zeros((SPEC, LAT))
+    taps = np.zeros((8, SPEC))
+    shift = np.arange(TAPS) - HALO
+    field_f[:, 0] = field_b[:, 0] = 1.0
+    back_f[0] = back_b[0] = 1.0 / PERIOD
+    taps[:TAPS, 0] = 1.0
+    half = PERIOD // 2
+    for f in range(1, half + 1):
+        one, two, three = f, half + f, 2 * half + f
+        cos, sin = np.cos(angle * f * row), np.sin(angle * f * row)
+        c, d = np.cos(angle * f * shift), np.sin(angle * f * shift)
+        taps[:TAPS, one], taps[:TAPS, two], taps[:TAPS, three] = c, d - c, c + d
+        field_f[:, one], field_f[:, two], field_f[:, three] = cos - sin, cos, -sin
+        field_b[:, one], field_b[:, two], field_b[:, three] = cos + sin, cos, sin
+        scale = 2.0 / PERIOD
+        back_f[one], back_f[two], back_f[three] = scale * (cos - sin), -scale * sin, -scale * cos
+        back_b[one], back_b[two], back_b[three] = scale * (cos + sin), scale * sin, -scale * cos
+
+    def stacked(values):
+        return np.concatenate(split_constant(values), axis=0)
+
+    def beside(values):
+        return np.concatenate(split_constant(values), axis=1)
+
+    spread_high, spread_low = np.zeros((64, TAPS * SPEC)), np.zeros((64, TAPS * SPEC))
+    high, low = split_constant(taps)
+    for a in range(TAPS):
+        spread_high[8 * a : 8 * a + 8, a * SPEC : (a + 1) * SPEC] = high
+        spread_low[8 * a : 8 * a + 8, a * SPEC : (a + 1) * SPEC] = low
+    spread = np.concatenate([spread_high, spread_high, spread_low]).astype(BF)
+    gather = np.zeros((SPEC, LAT))
+    gather[:, :8] = taps.T
+    return (
+        stacked(field_f),
+        np.concatenate([stacked(back_f.T), stacked(field_b)], axis=1),
+        beside(back_f),
+        beside(back_b),
+        spread,
+        beside(gather),
+    )
 
 
 def column(ref, at):
@@ -58,7 +109,13 @@
     taps_ref,
     gain_ref,
     win_ref,
-    wout_ref,
+    wout_t,
+    field_f,
+    field_g,
+    back_f,
+    back_b,
+    spread,
+    gather,
     sout_ref,
     gin_ref,
     gwin_ref,
@@ -69,21 +126,17 @@
     c32,
     xa,
     ga,
-    xf,
-    kb,
+    xh,
+    gh,
+    gw,
     kf,
+    dkf,
     flat_taps,
-    spread_to,
-    mixed_buf,
+    sum_high,
+    sum_low,
     gainb,
     win_t,
-    wout_t,
-    shift_b,
-    shift_g,
-    pick,
-    ybuf,
-    gshift,
-    prod,
+    wout,
     hid_buf,
     gp_buf,
     acc_in,
@@ -148,7 +201,6 @@
     x32[...] = state_ref[...].astype(F32).reshape(C * LON, LAT)
     for i in (13, 14, 15, 0, 1, 2):
         own = column(x32, i)
-        xf[HALO + i] = own
         xa[HALO + i] = own.astype(BF)
     if remote:
         pl.semaphore_wait(barrier, len(peers))
@@ -157,87 +209,60 @@
             one.start()
     for i in range(3, 13):
         own = column(x32, i)
-        xf[HALO + i] = own
         xa[HALO + i] = own.astype(BF)
     c32[...] = cot_ref[...].astype(F32).reshape(C * LON, LAT)
 
-    taps = TAPS * TAPS
     flat_taps[...] = jnp.zeros_like(flat_taps)
     for a in range(TAPS):
-        flat_taps[:, 8 * a : 8 * a + TAPS] = taps_ref[:, a, :]
-    rest = flat_taps[...]
-    pieces = []
-    for _ in range(3):
-        piece = rest.astype(BF)
-        pieces.append(piece)
-        rest = rest - piece.astype(F32)
-    split = jnp.concatenate(pieces, axis=1)
-    place = lax.broadcasted_iota(jnp.int32, (3 * LAT, LAT), 0) % LAT
-    for a in range(TAPS):
-        for b in range(TAPS):
-            t = a * TAPS + b
-            spread_to[:, t * LAT : (t + 1) * LAT] = one_hot(place == 8 * a + b)
-    kf[...] = matmul(split, spread_to[...])
-    for t in range(taps):
-        kb[t] = kf[:, t * LAT : (t + 1) * LAT].astype(BF)
+        flat_taps[8 * a : 8 * a + TAPS, 0:C] = taps_ref[a]
+    rest = flat_taps[...].T[0:C, :]
+    high = rest.astype(BF)
+    low = (rest - high.astype(F32)).astype(BF)
+    kf[...] = matmul(
+        jnp.concatenate([high[:, 0:64], low[:, 0:64], high[:, 0:64]], axis=1), spread[...]
+    )
     gainb[...] = jnp.broadcast_to(gain_ref[...], (LAT, C)).T
     win_t[...] = win_ref[...].T
-    wout_t[...] = wout_ref[...].T
-    rows = lax.broadcasted_iota(jnp.int32, (LAT, LAT), 0)
-    lanes = lax.broadcasted_iota(jnp.int32, (LAT, LAT), 1)
-    for b in range(TAPS):
-        backward = one_hot(rows == lanes - (b - HALO))
-        shift_b[b * LAT : (b + 1) * LAT, :] = backward
-        shift_g[:, b * LAT : (b + 1) * LAT] = backward
-    for t in range(TAPS * TAPS + 1):
-        pick[t * LAT : (t + 1) * LAT, :] = one_hot(lanes == t)
-
+    wout[...] = wout_t[...].T
     acc_in[...] = jnp.zeros_like(acc_in)
     acc_out[...] = jnp.zeros_like(acc_out)
     acc_gain[...] = jnp.zeros_like(acc_gain)
 
-    def filtered(field, col, flip, shifts):
+    def doubled(columns):
+        flat = columns.reshape(-1, LAT)
+        return jnp.concatenate([flat, flat], axis=1)
+
+    def field_spectrum(at, count):
+        spectrum = matmul(doubled(xa[at : at + count]), field_f[...])
+        xh[at : at + count] = spectrum.reshape(count, C, SPEC)
+
+    def grad_spectrum(at, count):
+        spectrum = matmul(doubled(ga[at : at + count]), field_g[:, SPEC:])
+        gh[at : at + count] = spectrum.reshape(count, C, SPEC)
+
+    def filtered(field, col, flip, inverse):
         def one_tile(tile, carry):
             at = pl.multiple_of(tile * TILE, TILE)
-            window = field[pl.ds(col, GROUP + 2 * HALO), pl.ds(at, TILE), :]
-            for b in range(TAPS):
+            for half in range(0, SPEC, LAT):
+                window = field[pl.ds(col, GROUP + 2 * HALO), pl.ds(at, TILE), half : half + LAT]
                 terms = []
                 for a in range(TAPS):
                     first = 2 * HALO - a if flip else a
-                    weight = kb[a * TAPS + b, pl.ds(at, TILE), :]
+                    lane = a * SPEC + half
+                    weight = kf[pl.ds(at, TILE), lane : lane + LAT]
                     terms.append(weight[None] * window[first : first + GROUP])
-                ybuf[:, pl.ds(at, TILE), b * LAT : (b + 1) * LAT] = tree_sum(terms)
+                total = tree_sum(terms)
+                high = total.astype(BF)
+                sum_high[:, pl.ds(at, TILE), half : half + LAT] = high
+                sum_low[:, pl.ds(at, TILE), half : half + LAT] = (
+                    total - high.astype(F32)
+                ).astype(BF)
             return carry
 
         lax.fori_loop(0, C // TILE, one_tile, 0)
-        flat = ybuf[...].reshape(GROUP * C, TAPS * LAT)
-        return matmul(flat, shifts[...]).reshape(GROUP, C, LAT)
-
-    def filtered_exact(col):
-        lane = lax.broadcasted_iota(jnp.int32, (GROUP, 8, LAT), 2)
-
-        def one_tile(tile, carry):
-            at = pl.multiple_of(tile * 8, 8)
-            window = xf[pl.ds(col, GROUP + 2 * HALO), pl.ds(at, 8), :]
-            total = None
-            for b in range(TAPS):
-                terms = [
-                    kf[pl.ds(at, 8), (a * TAPS + b) * LAT : (a * TAPS + b + 1) * LAT][None]
-                    * window[a : a + GROUP]
-                    for a in range(TAPS)
-                ]
-                part = tree_sum(terms)
-                by = b - HALO
-                if by != 0:
-                    turned = pltpu.roll(part, (-by) % LAT, axis=2)
-                    inside = lane < LAT - by if by > 0 else lane >= -by
-                    part = jnp.where(inside, turned, 0.0)
-                total = part if total is None else total + part
-            mixed_buf[:, pl.ds(at, 8), :] = total
-            return carry
-
-        lax.fori_loop(0, C // 8, one_tile, 0)
-        return mixed_buf[...]
+        main = matmul(sum_high[...].reshape(GROUP * C, SPEC), inverse[...])
+        rest = matmul(sum_low[...].reshape(GROUP * C, SPEC), inverse[:, 0:LAT])
+        return (main[:, 0:LAT] + main[:, LAT:] + rest).reshape(GROUP, C, LAT)
 
     def masks(col):
         return [sea_ref[pl.ds(col + k, 1), :].astype(F32) for k in range(GROUP)]
@@ -246,7 +271,7 @@
         return jnp.concatenate([parts[k] for k in range(GROUP)], axis=1)
 
     def forward_group(col):
-        mixed = filtered_exact(col)
+        mixed = filtered(xh, col, False, back_f)
         centred = mixed - jnp.mean(mixed, axis=1, keepdims=True)
         variance = jnp.mean(centred * centred, axis=1, keepdims=True)
         inv_scale = lax.rsqrt(variance + 1e-06)
@@ -258,7 +283,7 @@
         block = 128
         for h in range(0, HID, block):
             pre = matmul(win_t[h : h + block, :], normed)
-            grad_hidden = matmul(wout_ref[h : h + block, :], grad_out)
+            grad_hidden = matmul(wout[h : h + block, :], grad_out)
             square = pre * pre
             inner = pre * (0.7978845608028654 + 0.035677408136300125 * square)
             gate = 0.5 + 0.5 * jnp.tanh(inner)
@@ -283,11 +308,15 @@
             first = jnp.mean(grad_scaled, axis=0, keepdims=True)
             second = jnp.mean(product * gain, axis=0, keepdims=True)
             grad_conv = inv_scale[k] * (grad_scaled - first - scaled[k] * second)
-            ga[HALO + col + k] = grad_conv.astype(BF)
+            grad_conv = grad_conv.astype(BF)
+            ga[HALO + col + k] = grad_conv
+            spectrum = matmul(doubled(grad_conv), field_g[...])
+            gw[col + k] = spectrum[:, 0:SPEC]
+            gh[HALO + col + k] = spectrum[:, SPEC:]
 
     def fill_halo():
-        for i in (0, 1, 2, 19, 20, 21):
-            xf[i] = xa[i].astype(F32)
+        field_spectrum(0, HALO)
+        field_spectrum(LON + HALO, HALO)
 
     def one_group(step, carry):
         if remote:
@@ -301,6 +330,8 @@
         forward_group(lax.rem(GROUP + step * GROUP, LON))
         return carry
 
+    for at in range(HALO, LON + HALO, GROUP):
+        field_spectrum(at, GROUP)
     if not remote:
         local_halo(xa)
         fill_halo()
@@ -312,6 +343,8 @@
             one.start()
     else:
         local_halo(ga)
+        grad_spectrum(0, HALO)
+        grad_spectrum(LON + HALO, HALO)
 
     for o in range(16):
         at = OWN * o
@@ -377,30 +410,30 @@
         )
         w_core()
 
-    def shifted(i, carry):
-        gshift[i] = matmul(ga[HALO + i], shift_g[...]).astype(BF)
+    if remote:
+        w_owners()
+
+    def products(tile, carry):
+        at = pl.multiple_of(tile * 8, 8)
+        for half in range(0, SPEC, LAT):
+            grads = gw[:, pl.ds(at, 8), half : half + LAT]
+            for a in range(TAPS):
+                terms = grads * xh[a : a + LON, pl.ds(at, 8), half : half + LAT]
+                lane = a * SPEC + half
+                dkf[pl.ds(at, 8), lane : lane + LAT] = jnp.sum(terms, axis=0)
         return carry
 
-    lax.fori_loop(0, LON, shifted, 0)
-    if remote:
-        w_owners()
-
-    def products(tile, carry):
-        at = pl.multiple_of(tile * TILE, TILE)
-        for b in range(TAPS):
-            grads = gshift[:, pl.ds(at, TILE), b * LAT : (b + 1) * LAT]
-            for a in range(TAPS):
-                field = xa[a : a + LON, pl.ds(at, TILE), :]
-                terms = grads * field
-                t = a * TAPS + b
-                prod[pl.ds(at, TILE), t * LAT : (t + 1) * LAT] = tree_sum(
-                    [terms[k] for k in range(LON)]
-                )
-        return carry
-
-    lax.fori_loop(0, C // TILE, products, 0)
-    prod[:, TAPS * TAPS * LAT :] = acc_gain[...].astype(BF)
-    dks[0:C, :] = matmul(prod[...], pick[...])
+    lax.fori_loop(0, C // 8, products, 0)
+    lanes = lax.broadcasted_iota(jnp.int32, (C, LAT), 1)
+    total = jnp.where(lanes == TAPS * TAPS, jnp.sum(acc_gain[...], axis=1, keepdims=True), 0.0)
+    for a in range(TAPS):
+        part = dkf[:, a * SPEC : (a + 1) * SPEC]
+        high = part.astype(BF)
+        low = (part - high.astype(F32)).astype(BF)
+        both = matmul(high, gather[...])
+        found = both[:, 0:LAT] + both[:, LAT:] + matmul(low, gather[:, 0:LAT])
+        total = total + (pltpu.roll(found, a * TAPS, axis=1) if a else found)
+    dks[0:C, :] = total
     dks[C : C + 16, :] = jnp.zeros((16, LAT), F32)
     for o in range(16):
         ksend[o % 2, o // 2] = dks[OWN * o : OWN * o + 16, :]
@@ -408,11 +441,11 @@
         k_core()
 
     def backward_group(col):
-        spread = filtered(ga, col, True, shift_b)
+        moved = filtered(gh, col, True, back_b)
         mask = masks(col)
         for k in range(GROUP):
             at = pl.ds(col + k, C, stride=LON)
-            c32[at, :] = c32[at, :] * mask[k] + spread[k]
+            c32[at, :] = c32[at, :] * mask[k] + moved[k]
 
     def one_back(step, carry):
         backward_group(lax.rem(GROUP + step * GROUP, LON))
@@ -425,6 +458,8 @@
         k_owners()
         for one in g_halo:
             one.wait()
+        grad_spectrum(0, HALO)
+        grad_spectrum(LON + HALO, HALO)
     lax.fori_loop(2, 4, one_back, 0)
     if remote:
         k_slabs()
@@ -438,13 +473,28 @@
         small = ksend[0, 0] * factor
     wide = HID // 2
     gwin_ref[...] = weights[0:12, 0:HID]
-    stage[0, 0:4, 0:HID] = weights[12:16, 0:HID]
-    stage[0, 4:12, 0:wide] = weights[0:8, HID:PACKED]
-    stage[0, 4:12, wide:HID] = weights[8:16, HID:PACKED]
-    gwout_ref[...] = stage[0, :, 0:HID].T[:, 0:OWN]
+    gwout_ref[0:4, :] = weights[12:16, 0:HID]
+    gwout_ref[4:12, 0:wide] = weights[0:8, HID:PACKED]
+    gwout_ref[4:12, wide:HID] = weights[8:16, HID:PACKED]
+    small_t = small.T
     for a in range(TAPS):
-        gk_ref[:, a, :] = small[0:OWN, a * TAPS : (a + 1) * TAPS]
-    gg_ref[...] = small.T[TAPS * TAPS : TAPS * TAPS + 1, 0:OWN]
+        gk_ref[a] = small_t[a * TAPS : (a + 1) * TAPS, 0:OWN]
+    gg_ref[...] = small_t[TAPS * TAPS : TAPS * TAPS + 1, 0:OWN]
+
+
+def deliver(*refs):
+    count = len(refs) // 3
+    sems = refs[-1]
+    sources, targets, held = refs[:count], refs[count : 2 * count], refs[2 * count : 3 * count]
+    arrive = [pltpu.make_async_copy(sources[k], held[k], sems.at[0, k]) for k in range(count)]
+    leave = [pltpu.make_async_copy(held[k], targets[k], sems.at[1, k]) for k in range(count)]
+    for one in arrive:
+        one.start()
+    for k in range(count):
+        arrive[k].wait()
+        leave[k].start()
+    for one in leave:
+        one.wait()
 
 
 def block(n_lon, n_sample, factor, state, cot, sea, taps, gain, win, wout):
@@ -454,8 +504,8 @@
         shape((C, LON, LAT), BF),
         shape((C, LON, LAT), BF),
         shape((OWN, HID), F32),
-        shape((HID, OWN), F32),
-        shape((OWN, TAPS, TAPS), F32),
+        shape((OWN, HID), F32),
+        shape((TAPS, TAPS, OWN), F32),
         shape((1, OWN), F32),
     )
     scratch = [
@@ -463,21 +513,17 @@
         pltpu.VMEM((C * LON, LAT), F32),
         pltpu.VMEM((LON + 2 * HALO, C, LAT), BF),
         pltpu.VMEM((LON + 2 * HALO, C, LAT), BF),
-        pltpu.VMEM((LON + 2 * HALO, C, LAT), F32),
-        pltpu.VMEM((TAPS * TAPS, C, LAT), BF),
-        pltpu.VMEM((C, TAPS * TAPS * LAT), F32),
-        pltpu.VMEM((C, LAT), F32),
-        pltpu.VMEM((3 * LAT, TAPS * TAPS * LAT), BF),
-        pltpu.VMEM((GROUP, C, LAT), F32),
+        pltpu.VMEM((LON + 2 * HALO, C, SPEC), F32),
+        pltpu.VMEM((LON + 2 * HALO, C, SPEC), F32),
+        pltpu.VMEM((LON, C, SPEC), F32),
+        pltpu.VMEM((C, TAPS * SPEC), F32),
+        pltpu.VMEM((C, TAPS * SPEC), F32),
+        pltpu.VMEM((LAT, 2 * LAT), F32),
+        pltpu.VMEM((GROUP, C, SPEC), BF),
+        pltpu.VMEM((GROUP, C, SPEC), BF),
         pltpu.VMEM((C, LAT), F32),
         pltpu.VMEM((HID, C), BF),
-        pltpu.VMEM((C, HID), BF),
-        pltpu.VMEM((TAPS * LAT, LAT), BF),
-        pltpu.VMEM((LAT, TAPS * LAT), BF),
-        pltpu.VMEM(((TAPS * TAPS + 1) * LAT, LAT), BF),
-        pltpu.VMEM((GROUP, C, TAPS * LAT), BF),
-        pltpu.VMEM((LON, C, TAPS * LAT), BF),
-        pltpu.VMEM((C, (TAPS * TAPS + 1) * LAT), BF),
+        pltpu.VMEM((HID, C), BF),
         pltpu.VMEM((HID, GROUP * LAT), BF),
         pltpu.VMEM((HID, GROUP * LAT), BF),
         pltpu.VMEM((C, HID), F32),
@@ -499,10 +545,10 @@
         pltpu.SemaphoreType.DMA((34,)),
     ]
     extra = dict(collective_id=0, has_side_effects=True) if n_lon > 1 else {}
-    return pl.pallas_call(
+    results = pl.pallas_call(
         functools.partial(kernel_body, n_lon, n_sample, factor),
         out_shape=outs,
-        in_specs=[vmem] * 7,
+        in_specs=[vmem] * 13,
         out_specs=(vmem,) * 6,
         scratch_shapes=scratch,
         compiler_params=pltpu.CompilerParams(vmem_limit_bytes=60 * 1024 * 1024, **extra),
@@ -510,11 +556,21 @@
         state.reshape(C, LON, LAT),
         cot.reshape(C, LON, LAT),
         sea,
-        taps,
+        taps.transpose(1, 2, 0),
         gain.reshape(1, C),
         win,
-        wout,
+        wout.T,
+        *spectral_constants(),
     )
+    anywhere = pl.BlockSpec(memory_space=pl.ANY)
+    return pl.pallas_call(
+        deliver,
+        out_shape=outs,
+        in_specs=[anywhere] * 6,
+        out_specs=(anywhere,) * 6,
+        scratch_shapes=[pltpu.VMEM(out.shape, out.dtype) for out in outs]
+        + [pltpu.SemaphoreType.DMA((2, 6))],
+    )(*results)
 
 
 def solution(mesh):
@@ -528,8 +584,8 @@
             out[0].reshape(shape),
             out[1].reshape(shape),
             out[2],
-            out[3],
-            out[4],
+            out[3].T,
+            out[4].transpose(2, 0, 1),
             out[5].reshape(OWN),
         )
 

time: 72.3 us -> 53.3 us (0.74)
  local copies, waits for them, and re-layouts: 10.6 us -> 0 us
  Pallas kernels: 60.7 us -> 52.5 us
    pallas_call x1, Pallas kernels: 60.7 us -> 50.1 us  [block(): pl.pallas_call(functools.partial(kernel_body, n_lon, n_sample, factor), o...]
    unnamed x16 -> x0, local copies, waits for them, and re-layouts: 10.6 us -> none
    pallas_call x0 -> x1, Pallas kernels: none -> 2.4 us  [block(): pl.pallas_call(deliver, out_shape=outs, in_specs=[anywhere] * 6, out_spec...]
where the time goes in v2:
time: 53.3 us; the launch traced here: 53.1 us
  Pallas kernels  52.5 us (98%)
  between operations  0.64 us (1%)
    pallas_call x1, Pallas kernels, block(): pl.pallas_call(functools.partial(kernel_body, n_lon, n_sample, factor), o...  50.1 us
    pallas_call x1, Pallas kernels, block(): pl.pallas_call(deliver, out_shape=outs, in_specs=[anywhere] * 6, out_spec...  2.4 us

profile of v2, /device:TPU:0, one launch (start us, length us, event | category | flops | bytes accessed | tf_op | source)
XLA Modules:
  0.0 53.1 jit_solution(12345697755719810152)
XLA Ops:
  0.6 50.1 %shard_map.172 = (bf16[192,16,128]{2,1,0:T(8,128)(2,1)}, bf16[192,16,128]{2,1,0:T(8,128)(2,1)}, f32[12,768]{1,0:T(8,128)}, f32[12,768]{1,0:T(8,128)}, f32[7,7,12]{2,1,0:T(8,128)}, /*index=5*/f32[1,12]{1,0:T(1,128)}) custom-call(bf16[192,16,128]{2,1,0:T(8,128)(2,1)} %bitcast.10, bf16[192,16,128]{2,1,0:T(8,128)(2,1)} %bitcast.11, s32[16,128]{1,0:T(8,128)} %sea_ref.1, ...), custom_call_target="tpu_custom_call" | custom-call | tf_op jit(solution)/shard_map/pallas_call | solution.py:548
  50.7 2.4 %shard_map.173 = (bf16[192,16,128]{2,1,0:T(8,128)(2,1)}, bf16[192,16,128]{2,1,0:T(8,128)(2,1)}, f32[12,768]{1,0:T(8,128)}, f32[12,768]{1,0:T(8,128)}, f32[7,7,12]{2,1,0:T(8,128)}, /*index=5*/f32[1,12]{1,0:T(1,128)}) custom-call(bf16[192,16,128]{2,1,0:T(8,128)(2,1)} %get-tuple-element.18.refs_0_, bf16[192,16,128]{2,1,0:T(8,128)(2,1)} %get-tuple-element.19.refs_1_, ...), custom_call_target="tpu_custom_call" | custom-call | tf_op jit(solution)/shard_map/pallas_call | solution.py:566

commit v3 on v2

--- a/solution.py
+++ b/solution.py
@@ -18,9 +18,12 @@
 TAPS = 7
 HALO = 3
 GROUP = 4
+HID_BLOCK = 128
+CELL_BLOCK = 512
 TILE = 16
 OWN = 12
 PACKED = 1152
+PIECES = PACKED // LAT
 BF = jnp.bfloat16
 F32 = jnp.float32
 MESH = pl.DeviceIdType.MESH
@@ -137,8 +140,12 @@
     gainb,
     win_t,
     wout,
-    hid_buf,
-    gp_buf,
+    norm_all,
+    cot_all,
+    hid_all,
+    gp_all,
+    scaled_all,
+    inv_all,
     acc_in,
     acc_out,
     acc_gain,
@@ -148,6 +155,8 @@
     wcore,
     wmid,
     wparts,
+    bsend,
+    bparts,
     wslab,
     ksend,
     kcore,
@@ -224,8 +233,6 @@
     gainb[...] = jnp.broadcast_to(gain_ref[...], (LAT, C)).T
     win_t[...] = win_ref[...].T
     wout[...] = wout_t[...].T
-    acc_in[...] = jnp.zeros_like(acc_in)
-    acc_out[...] = jnp.zeros_like(acc_out)
     acc_gain[...] = jnp.zeros_like(acc_gain)
 
     def doubled(columns):
@@ -270,45 +277,59 @@
     def side_by_side(parts):
         return jnp.concatenate([parts[k] for k in range(GROUP)], axis=1)
 
+    def lanes_of(col):
+        return pl.ds(pl.multiple_of(col * LAT, GROUP * LAT), GROUP * LAT)
+
     def forward_group(col):
         mixed = filtered(xh, col, False, back_f)
         centred = mixed - jnp.mean(mixed, axis=1, keepdims=True)
         variance = jnp.mean(centred * centred, axis=1, keepdims=True)
         inv_scale = lax.rsqrt(variance + 1e-06)
         scaled = centred * inv_scale
-        gain = gainb[...]
-        normed = side_by_side((scaled * gain[None]).astype(BF))
+        scaled_all[pl.ds(col, GROUP)] = scaled
+        inv_all[pl.ds(col, GROUP), :] = inv_scale.reshape(GROUP, LAT)
+        normed = side_by_side((scaled * gainb[...][None]).astype(BF))
         mask = masks(col)
         grad_out = side_by_side([(column(c32, col + k) * mask[k]).astype(BF) for k in range(GROUP)])
-        block = 128
-        for h in range(0, HID, block):
-            pre = matmul(win_t[h : h + block, :], normed)
-            grad_hidden = matmul(wout[h : h + block, :], grad_out)
-            square = pre * pre
-            inner = pre * (0.7978845608028654 + 0.035677408136300125 * square)
-            gate = 0.5 + 0.5 * jnp.tanh(inner)
-            hidden = pre * gate
-            slope = gate + hidden * (1.0 - gate) * (
-                1.5957691216057308 + 0.21406444881780074 * square
-            )
-            hid_buf[h : h + block, :] = hidden.astype(BF)
-            gp_buf[h : h + block, :] = (grad_hidden * slope).astype(BF)
-        branch = matmul(wout_t[...], hid_buf[...])
-        grad_normed = matmul(win_ref[...], gp_buf[...])
-        acc_out[...] += matmul_nt(grad_out, hid_buf[...])
-        acc_in[...] += matmul_nt(normed, gp_buf[...])
+        where = lanes_of(col)
+        norm_all[:, where] = normed
+        cot_all[:, where] = grad_out
+        for h in range(0, HID, HID_BLOCK):
+            for n in range(0, GROUP * LAT, CELL_BLOCK):
+                pre = matmul(win_t[h : h + HID_BLOCK, :], normed[:, n : n + CELL_BLOCK])
+                grad_hidden = matmul(wout[h : h + HID_BLOCK, :], grad_out[:, n : n + CELL_BLOCK])
+                square = pre * pre
+                inner = pre * (0.7978845608028654 + 0.035677408136300125 * square)
+                gate = 0.5 + 0.5 * jnp.tanh(inner)
+                hidden = pre * gate
+                slope = gate + hidden * (1.0 - gate) * (
+                    1.5957691216057308 + 0.21406444881780074 * square
+                )
+                at = pl.ds(pl.multiple_of(col * LAT + n, CELL_BLOCK), CELL_BLOCK)
+                hid_all[h : h + HID_BLOCK, at] = hidden.astype(BF)
+                gp_all[h : h + HID_BLOCK, at] = (grad_hidden * slope).astype(BF)
+
+    def backward_mlp(col):
+        where = lanes_of(col)
+        gain = gainb[...]
+        mask = masks(col)
+        branch = matmul(wout_t[...], hid_all[:, where])
         for k in range(GROUP):
             lane = slice(k * LAT, (k + 1) * LAT)
             at = pl.ds(col + k, C, stride=LON)
             x32[at, :] = mask[k] * (x32[at, :] + branch[:, lane])
+        grad_normed = matmul(win_ref[...], gp_all[:, where])
+        for k in range(GROUP):
+            lane = slice(k * LAT, (k + 1) * LAT)
+            scaled = scaled_all[col + k]
             grad = grad_normed[:, lane]
-            product = grad * scaled[k]
+            product = grad * scaled
             acc_gain[...] += product
             grad_scaled = grad * gain
             first = jnp.mean(grad_scaled, axis=0, keepdims=True)
             second = jnp.mean(product * gain, axis=0, keepdims=True)
-            grad_conv = inv_scale[k] * (grad_scaled - first - scaled[k] * second)
-            grad_conv = grad_conv.astype(BF)
+            inv_scale = inv_all[pl.ds(col + k, 1), :]
+            grad_conv = (inv_scale * (grad_scaled - first - scaled * second)).astype(BF)
             ga[HALO + col + k] = grad_conv
             spectrum = matmul(doubled(grad_conv), field_g[...])
             gw[col + k] = spectrum[:, 0:SPEC]
@@ -318,100 +339,91 @@
         field_spectrum(0, HALO)
         field_spectrum(LON + HALO, HALO)
 
-    def one_group(step, carry):
-        if remote:
-
-            @pl.when(step == 2)
-            def _():
-                for one in x_halo:
-                    one.wait()
-                fill_halo()
-
-        forward_group(lax.rem(GROUP + step * GROUP, LON))
-        return carry
+    def in_groups(first, last, work):
+        def one_group(step, carry):
+            work(lax.rem(GROUP + step * GROUP, LON))
+            return carry
+
+        lax.fori_loop(first, last, one_group, 0)
+
+    def start(copies):
+        for one in copies:
+            one.start()
+
+    def wait(copies):
+        for one in copies:
+            one.wait()
 
     for at in range(HALO, LON + HALO, GROUP):
         field_spectrum(at, GROUP)
-    if not remote:
+    in_groups(0, 2, forward_group)
+    if remote:
+        wait(x_halo)
+    else:
         local_halo(xa)
-        fill_halo()
-    lax.fori_loop(0, LON // GROUP, one_group, 0)
-
-    if remote:
-        g_halo = halo_copies(ga, 2)
-        for one in g_halo:
-            one.start()
-    else:
-        local_halo(ga)
-        grad_spectrum(0, HALO)
-        grad_spectrum(LON + HALO, HALO)
-
+    fill_halo()
+    in_groups(2, 4, forward_group)
+
+    acc_out[...] = matmul_nt(cot_all[...], hid_all[...])
+    acc_in[...] = matmul_nt(norm_all[...], gp_all[...])
+    wide = HID // 2
     for o in range(16):
         at = OWN * o
-        wide = HID // 2
         stage[o, 0:12, 0:HID] = acc_in[at : at + 12, :]
         stage[o, 12:16, 0:HID] = acc_out[at : at + 4, :]
         stage[o, 0:8, HID:PACKED] = acc_out[at + 4 : at + 12, 0:wide]
         stage[o, 8:16, HID:PACKED] = acc_out[at + 4 : at + 12, wide:HID]
     for o in range(16):
-        wsend[o % 2, o // 2] = stage[o].astype(BF)
-
-    def reduction(base, packed, from_core, middle, parts, slab, kind):
-        def core_copy():
-            return copy(packed.at[1 - core], from_core, base, partner)
-
-        def owner_copies():
+        q = o // 2
+        for t in range(PIECES):
+            slot = q if t < 8 else 8
+            piece = stage[o, :, t * LAT : (t + 1) * LAT].astype(BF)
+            wsend[o % 2, (q + t) % 8, slot] = piece
+
+    if remote:
+
+        def to_slabs(source, target, base):
             return [
-                copy(middle.at[other], parts.at[d], base + 1 + d, {"sample": 2 * other + core})
+                copy(source(other), target(d), base + d, {"lon": other})
+                for d, other in enumerate(slabs)
+            ]
+
+        def to_owners(source, target, base):
+            return [
+                copy(source.at[other], target.at[d], base + d, {"sample": 2 * other + core})
                 for d, other in enumerate(owners)
             ]
 
-        def slab_copies():
-            return [
-                copy(slab.at[lon], slab.at[lon], base + 1 + len(owners) + d, {"lon": other})
-                for d, other in enumerate(slabs)
-            ]
-
-        def start_core():
-            core_copy().start()
-
-        def start_owners():
-            core_copy().wait()
-            middle[...] = (packed[core].astype(F32) + from_core[...].astype(F32)).astype(kind)
-            for one in owner_copies():
-                one.start()
-
-        def start_slabs():
-            for one in owner_copies():
-                one.wait()
-            total = middle[owner].astype(F32)
-            for d in range(len(owners)):
-                total = total + parts[d].astype(F32)
-            slab[lon] = total.astype(kind)
-            for one in slab_copies():
-                one.start()
-
-        def finish():
-            for one in slab_copies():
-                one.wait()
-            total = slab[0].astype(F32)
-            for other in range(1, n_lon):
-                total = total + slab[other].astype(F32)
-            return total * factor
-
-        return start_core, start_owners, start_slabs, finish
-
-    if remote:
-        w_core, w_owners, w_slabs, w_finish = reduction(
-            4, wsend, wcore, wmid, wparts, wslab, BF
-        )
-        k_core, k_owners, k_slabs, k_finish = reduction(
-            19, ksend, kcore, kmid, kparts, kslab, F32
-        )
-        w_core()
-
-    if remote:
-        w_owners()
+        def w_core():
+            return [copy(wsend.at[1 - core], wcore, 4, partner)]
+
+        def w_lon():
+            return to_slabs(lambda other: wmid.at[other], lambda d: wparts.at[d], 5)
+
+        def w_own():
+            return to_owners(bsend, bparts, 12)
+
+        def w_all():
+            return to_slabs(lambda other: wslab.at[lon], lambda d: wslab.at[lon], 19)
+
+        def k_core():
+            return [copy(ksend.at[1 - core], kcore, 26, partner)]
+
+        def k_own():
+            return to_owners(kmid, kparts, 27)
+
+        def k_all():
+            return to_slabs(lambda other: kslab.at[lon], lambda d: kslab.at[lon], 34)
+
+        start(w_core())
+    in_groups(2, 4, backward_mlp)
+    if remote:
+        g_halo = halo_copies(ga, 2)
+        start(g_halo)
+        wait(w_core())
+        wmid[...] = (wsend[core].astype(F32) + wcore[...].astype(F32)).astype(BF)
+        start(w_lon())
+    in_groups(0, 2, backward_mlp)
 
     def products(tile, carry):
         at = pl.multiple_of(tile * 8, 8)
@@ -438,7 +450,7 @@
     for o in range(16):
         ksend[o % 2, o // 2] = dks[OWN * o : OWN * o + 16, :]
     if remote:
-        k_core()
+        start(k_core())
 
     def backward_group(col):
         moved = filtered(gh, col, True, back_b)
@@ -447,31 +459,56 @@
             at = pl.ds(col + k, C, stride=LON)
             c32[at, :] = c32[at, :] * mask[k] + moved[k]
 
-    def one_back(step, carry):
-        backward_group(lax.rem(GROUP + step * GROUP, LON))
-        return carry
-
-    if remote:
-        w_slabs()
-    lax.fori_loop(0, 2, one_back, 0)
-    if remote:
-        k_owners()
-        for one in g_halo:
-            one.wait()
-        grad_spectrum(0, HALO)
-        grad_spectrum(LON + HALO, HALO)
-    lax.fori_loop(2, 4, one_back, 0)
-    if remote:
-        k_slabs()
+    if remote:
+        wait(w_lon())
+        total = wmid[lon].astype(F32)
+        for d in range(len(slabs)):
+            total = total + wparts[d].astype(F32)
+        for q in range(8):
+            bsend[q, 0] = total[q].astype(BF)
+            bsend[q, 1] = total[8].astype(BF)
+        start(w_own())
+    in_groups(0, 1, backward_group)
+    if remote:
+        wait(k_core())
+        kmid[...] = ksend[core] + kcore[...]
+        start(k_own())
+    in_groups(1, 2, backward_group)
+    if remote:
+        wait(w_own())
+        held = bsend[owner].astype(F32)
+        for d in range(len(owners)):
+            held = held + bparts[d].astype(F32)
+        wslab[lon] = held
+        start(w_all())
+        wait(g_halo)
+    else:
+        local_halo(ga)
+    grad_spectrum(0, HALO)
+    grad_spectrum(LON + HALO, HALO)
+    in_groups(2, 3, backward_group)
+    if remote:
+        wait(k_own())
+        held = kmid[owner]
+        for d in range(len(owners)):
+            held = held + kparts[d]
+        kslab[lon] = held
+        start(k_all())
+    in_groups(3, 4, backward_group)
     sout_ref[...] = x32[...].reshape(C, LON, LAT).astype(BF)
     gin_ref[...] = c32[...].reshape(C, LON, LAT).astype(BF)
     if remote:
-        weights = w_finish()
-        small = k_finish()
+        wait(w_all())
+        tiles = [wslab[lax.rem(owner + t, 8), 0] for t in range(8)] + [wslab[owner, 1]]
+        wait(k_all())
+        small = kslab[0]
+        for other in range(1, n_lon):
+            small = small + kslab[other]
     else:
-        weights = wsend[0, 0].astype(F32) * factor
-        small = ksend[0, 0] * factor
-    wide = HID // 2
+        tiles = [wsend[0, t % 8, 0 if t < 8 else 8].astype(F32) for t in range(PIECES)]
+        small = ksend[0, 0]
+    weights = jnp.concatenate(tiles, axis=1) * factor
+    small = small * factor
     gwin_ref[...] = weights[0:12, 0:HID]
     gwout_ref[0:4, :] = weights[12:16, 0:HID]
     gwout_ref[4:12, 0:wide] = weights[0:8, HID:PACKED]
@@ -524,25 +561,31 @@
         pltpu.VMEM((C, LAT), F32),
         pltpu.VMEM((HID, C), BF),
         pltpu.VMEM((HID, C), BF),
-        pltpu.VMEM((HID, GROUP * LAT), BF),
-        pltpu.VMEM((HID, GROUP * LAT), BF),
+        pltpu.VMEM((C, LON * LAT), BF),
+        pltpu.VMEM((C, LON * LAT), BF),
+        pltpu.VMEM((HID, LON * LAT), BF),
+        pltpu.VMEM((HID, LON * LAT), BF),
+        pltpu.VMEM((LON, C, LAT), F32),
+        pltpu.VMEM((LON, LAT), F32),
         pltpu.VMEM((C, HID), F32),
         pltpu.VMEM((C, HID), F32),
         pltpu.VMEM((C, LAT), F32),
         pltpu.VMEM((C + 16, LAT), F32),
         pltpu.VMEM((16, 16, PACKED), F32),
-        pltpu.VMEM((2, 8, 16, PACKED), BF),
-        pltpu.VMEM((8, 16, PACKED), BF),
-        pltpu.VMEM((8, 16, PACKED), BF),
-        pltpu.VMEM((7, 16, PACKED), BF),
-        pltpu.VMEM((8, 16, PACKED), BF),
+        pltpu.VMEM((2, 8, PIECES, 16, LAT), BF),
+        pltpu.VMEM((8, PIECES, 16, LAT), BF),
+        pltpu.VMEM((8, PIECES, 16, LAT), BF),
+        pltpu.VMEM((7, PIECES, 16, LAT), BF),
+        pltpu.VMEM((8, 2, 16, LAT), BF),
+        pltpu.VMEM((7, 2, 16, LAT), BF),
+        pltpu.VMEM((8, 2, 16, LAT), F32),
         pltpu.VMEM((2, 8, 16, LAT), F32),
         pltpu.VMEM((8, 16, LAT), F32),
         pltpu.VMEM((8, 16, LAT), F32),
         pltpu.VMEM((7, 16, LAT), F32),
         pltpu.VMEM((8, 16, LAT), F32),
-        pltpu.SemaphoreType.DMA((34,)),
-        pltpu.SemaphoreType.DMA((34,)),
+        pltpu.SemaphoreType.DMA((41,)),
+        pltpu.SemaphoreType.DMA((41,)),
     ]
     extra = dict(collective_id=0, has_side_effects=True) if n_lon > 1 else {}
     results = pl.pallas_call(

time: 53.3 us -> 52 us (0.976)
  Pallas kernels: 52.5 us -> 51.2 us
    pallas_call x1, Pallas kernels: 50.1 us -> 48.8 us  [block(): pl.pallas_call(functools.partial(kernel_body, n_lon, n_sample, factor), o...]
where the time goes in v3:
time: 52 us; the launch traced here: 51.9 us
  Pallas kernels  51.2 us (98%)
  between operations  0.64 us (1%)
    pallas_call x1, Pallas kernels, block(): pl.pallas_call(functools.partial(kernel_body, n_lon, n_sample, factor), o...  48.8 us
    pallas_call x1, Pallas kernels, block(): pl.pallas_call(deliver, out_shape=outs, in_specs=[anywhere] * 6, out_spec...  2.4 us

profile of v3, /device:TPU:0, one launch (start us, length us, event | category | flops | bytes accessed | tf_op | source)
XLA Modules:
  0.0 51.9 jit_solution(13258687766052912480)
XLA Ops:
  0.6 48.8 %shard_map.172 = (bf16[192,16,128]{2,1,0:T(8,128)(2,1)}, bf16[192,16,128]{2,1,0:T(8,128)(2,1)}, f32[12,768]{1,0:T(8,128)}, f32[12,768]{1,0:T(8,128)}, f32[7,7,12]{2,1,0:T(8,128)}, /*index=5*/f32[1,12]{1,0:T(1,128)}) custom-call(bf16[192,16,128]{2,1,0:T(8,128)(2,1)} %bitcast.10, bf16[192,16,128]{2,1,0:T(8,128)(2,1)} %bitcast.11, s32[16,128]{1,0:T(8,128)} %sea_ref.1, ...), custom_call_target="tpu_custom_call" | custom-call | tf_op jit(solution)/shard_map/pallas_call | solution.py:591
  49.5 2.4 %shard_map.173 = (bf16[192,16,128]{2,1,0:T(8,128)(2,1)}, bf16[192,16,128]{2,1,0:T(8,128)(2,1)}, f32[12,768]{1,0:T(8,128)}, f32[12,768]{1,0:T(8,128)}, f32[7,7,12]{2,1,0:T(8,128)}, /*index=5*/f32[1,12]{1,0:T(1,128)}) custom-call(bf16[192,16,128]{2,1,0:T(8,128)(2,1)} %get-tuple-element.18.refs_0_, bf16[192,16,128]{2,1,0:T(8,128)(2,1)} %get-tuple-element.19.refs_1_, ...), custom_call_target="tpu_custom_call" | custom-call | tf_op jit(solution)/shard_map/pallas_call | solution.py:609

commit v4 on v3

--- a/solution.py
+++ b/solution.py
@@ -18,12 +18,11 @@
 TAPS = 7
 HALO = 3
 GROUP = 4
-HID_BLOCK = 128
-CELL_BLOCK = 512
+HID_BLOCK = 256
+CELL_BLOCK = 256
 TILE = 16
 OWN = 12
 PACKED = 1152
-PIECES = PACKED // LAT
 BF = jnp.bfloat16
 F32 = jnp.float32
 MESH = pl.DeviceIdType.MESH
@@ -155,8 +154,6 @@
     wcore,
     wmid,
     wparts,
-    bsend,
-    bparts,
     wslab,
     ksend,
     kcore,
@@ -231,8 +228,8 @@
         jnp.concatenate([high[:, 0:64], low[:, 0:64], high[:, 0:64]], axis=1), spread[...]
     )
     gainb[...] = jnp.broadcast_to(gain_ref[...], (LAT, C)).T
-    win_t[...] = win_ref[...].T
-    wout[...] = wout_t[...].T
+    win_t[...] = (0.5 * win_ref[...].astype(F32)).astype(BF).T
+    wout[...] = (0.5 * wout_t[...].astype(F32)).astype(BF).T
     acc_gain[...] = jnp.zeros_like(acc_gain)
 
     def doubled(columns):
@@ -296,28 +293,30 @@
         cot_all[:, where] = grad_out
         for h in range(0, HID, HID_BLOCK):
             for n in range(0, GROUP * LAT, CELL_BLOCK):
-                pre = matmul(win_t[h : h + HID_BLOCK, :], normed[:, n : n + CELL_BLOCK])
-                grad_hidden = matmul(wout[h : h + HID_BLOCK, :], grad_out[:, n : n + CELL_BLOCK])
-                square = pre * pre
-                inner = pre * (0.7978845608028654 + 0.035677408136300125 * square)
-                gate = 0.5 + 0.5 * jnp.tanh(inner)
-                hidden = pre * gate
-                slope = gate + hidden * (1.0 - gate) * (
-                    1.5957691216057308 + 0.21406444881780074 * square
+                half = matmul(win_t[h : h + HID_BLOCK, :], normed[:, n : n + CELL_BLOCK])
+                grad_half = matmul(wout[h : h + HID_BLOCK, :], grad_out[:, n : n + CELL_BLOCK])
+                square = half * half
+                bent = jnp.tanh(half * (1.5957691216057308 + 0.28541926509040104 * square))
+                gate = 1.0 + bent
+                hidden = half * gate
+                slope = gate + hidden * (1.0 - bent) * (
+                    1.5957691216057308 + 0.8562577952712031 * square
                 )
                 at = pl.ds(pl.multiple_of(col * LAT + n, CELL_BLOCK), CELL_BLOCK)
                 hid_all[h : h + HID_BLOCK, at] = hidden.astype(BF)
-                gp_all[h : h + HID_BLOCK, at] = (grad_hidden * slope).astype(BF)
-
-    def backward_mlp(col):
-        where = lanes_of(col)
-        gain = gainb[...]
+                gp_all[h : h + HID_BLOCK, at] = (grad_half * slope).astype(BF)
+
+    def finish_state(col):
         mask = masks(col)
-        branch = matmul(wout_t[...], hid_all[:, where])
+        branch = matmul(wout_t[...], hid_all[:, lanes_of(col)])
         for k in range(GROUP):
             lane = slice(k * LAT, (k + 1) * LAT)
             at = pl.ds(col + k, C, stride=LON)
             x32[at, :] = mask[k] * (x32[at, :] + branch[:, lane])
+
+    def backward_mlp(col):
+        where = lanes_of(col)
+        gain = gainb[...]
         grad_normed = matmul(win_ref[...], gp_all[:, where])
         for k in range(GROUP):
             lane = slice(k * LAT, (k + 1) * LAT)
@@ -356,7 +355,29 @@
 
     for at in range(HALO, LON + HALO, GROUP):
         field_spectrum(at, GROUP)
+    def filter_grads(parts, fresh):
+        def one_tile(tile, carry):
+            at = pl.multiple_of(tile * 8, 8)
+            for half in range(0, SPEC, LAT):
+                lanes = slice(half, half + LAT)
+                for a in range(TAPS):
+                    spot = slice(a * SPEC + half, a * SPEC + half + LAT)
+                    total = 0.0 if fresh else dkf[pl.ds(at, 8), spot]
+                    for col, count in parts:
+                        grads = gw[col : col + count, pl.ds(at, 8), lanes]
+                        field = xh[col + a : col + a + count, pl.ds(at, 8), lanes]
+                        total = total + jnp.sum(grads * field, axis=0)
+                    dkf[pl.ds(at, 8), spot] = total
+            return carry
+
+        lax.fori_loop(0, C // 8, one_tile, 0)
+
     in_groups(0, 2, forward_group)
+    in_groups(0, 2, backward_mlp)
+    filter_grads([(GROUP, 2 * GROUP)], True)
+    cells = slice(GROUP * LAT, 3 * GROUP * LAT)
+    acc_out[...] = matmul_nt(cot_all[:, cells], hid_all[:, cells])
+    acc_in[...] = matmul_nt(norm_all[:, cells], gp_all[:, cells])
     if remote:
         wait(x_halo)
     else:
@@ -364,8 +385,9 @@
     fill_halo()
     in_groups(2, 4, forward_group)
 
-    acc_out[...] = matmul_nt(cot_all[...], hid_all[...])
-    acc_in[...] = matmul_nt(norm_all[...], gp_all[...])
+    for cells in (slice(0, GROUP * LAT), slice(3 * GROUP * LAT, LON * LAT)):
+        acc_out[...] += matmul_nt(cot_all[:, cells], hid_all[:, cells])
+        acc_in[...] += matmul_nt(norm_all[:, cells], gp_all[:, cells])
     wide = HID // 2
     for o in range(16):
         at = OWN * o
@@ -374,17 +396,13 @@
         stage[o, 0:8, HID:PACKED] = acc_out[at + 4 : at + 12, 0:wide]
         stage[o, 8:16, HID:PACKED] = acc_out[at + 4 : at + 12, wide:HID]
     for o in range(16):
-        q = o // 2
-        for t in range(PIECES):
-            slot = q if t < 8 else 8
-            piece = stage[o, :, t * LAT : (t + 1) * LAT].astype(BF)
-            wsend[o % 2, (q + t) % 8, slot] = piece
-
-    if remote:
-
-        def to_slabs(source, target, base):
+        wsend[o % 2, o // 2] = stage[o].astype(BF)
+
+    if remote:
+
+        def to_slabs(slab, base):
             return [
-                copy(source(other), target(d), base + d, {"lon": other})
+                copy(slab.at[lon], slab.at[lon], base + d, {"lon": other})
                 for d, other in enumerate(slabs)
             ]
 
@@ -397,23 +415,20 @@
         def w_core():
             return [copy(wsend.at[1 - core], wcore, 4, partner)]
 
-        def w_lon():
-            return to_slabs(lambda other: wmid.at[other], lambda d: wparts.at[d], 5)
-
         def w_own():
-            return to_owners(bsend, bparts, 12)
+            return to_owners(wmid, wparts, 5)
 
         def w_all():
-            return to_slabs(lambda other: wslab.at[lon], lambda d: wslab.at[lon], 19)
+            return to_slabs(wslab, 12)
 
         def k_core():
-            return [copy(ksend.at[1 - core], kcore, 26, partner)]
+            return [copy(ksend.at[1 - core], kcore, 19, partner)]
 
         def k_own():
-            return to_owners(kmid, kparts, 27)
+            return to_owners(kmid, kparts, 20)
 
         def k_all():
-            return to_slabs(lambda other: kslab.at[lon], lambda d: kslab.at[lon], 34)
+            return to_slabs(kslab, 27)
 
         start(w_core())
     in_groups(2, 4, backward_mlp)
@@ -422,20 +437,9 @@
         start(g_halo)
         wait(w_core())
         wmid[...] = (wsend[core].astype(F32) + wcore[...].astype(F32)).astype(BF)
-        start(w_lon())
-    in_groups(0, 2, backward_mlp)
-
-    def products(tile, carry):
-        at = pl.multiple_of(tile * 8, 8)
-        for half in range(0, SPEC, LAT):
-            grads = gw[:, pl.ds(at, 8), half : half + LAT]
-            for a in range(TAPS):
-                terms = grads * xh[a : a + LON, pl.ds(at, 8), half : half + LAT]
-                lane = a * SPEC + half
-                dkf[pl.ds(at, 8), lane : lane + LAT] = jnp.sum(terms, axis=0)
-        return carry
-
-    lax.fori_loop(0, C // 8, products, 0)
+        start(w_own())
+    filter_grads([(0, GROUP), (3 * GROUP, GROUP)], False)
+
     lanes = lax.broadcasted_iota(jnp.int32, (C, LAT), 1)
     total = jnp.where(lanes == TAPS * TAPS, jnp.sum(acc_gain[...], axis=1, keepdims=True), 0.0)
     for a in range(TAPS):
@@ -451,6 +455,11 @@
         ksend[o % 2, o // 2] = dks[OWN * o : OWN * o + 16, :]
     if remote:
         start(k_core())
+    in_groups(0, 4, finish_state)
+    if remote:
+        wait(k_core())
+        kmid[...] = ksend[core] + kcore[...]
+        start(k_own())
 
     def backward_group(col):
         moved = filtered(gh, col, True, back_b)
@@ -459,27 +468,13 @@
             at = pl.ds(col + k, C, stride=LON)
             c32[at, :] = c32[at, :] * mask[k] + moved[k]
 
-    if remote:
-        wait(w_lon())
-        total = wmid[lon].astype(F32)
-        for d in range(len(slabs)):
-            total = total + wparts[d].astype(F32)
-        for q in range(8):
-            bsend[q, 0] = total[q].astype(BF)
-            bsend[q, 1] = total[8].astype(BF)
-        start(w_own())
-    in_groups(0, 1, backward_group)
-    if remote:
-        wait(k_core())
-        kmid[...] = ksend[core] + kcore[...]
-        start(k_own())
-    in_groups(1, 2, backward_group)
+    in_groups(0, 2, backward_group)
     if remote:
         wait(w_own())
-        held = bsend[owner].astype(F32)
+        held = wmid[owner].astype(F32)
         for d in range(len(owners)):
-            held = held + bparts[d].astype(F32)
-        wslab[lon] = held
+            held = held + wparts[d].astype(F32)
+        wslab[lon] = held.astype(BF)
         start(w_all())
         wait(g_halo)
     else:
@@ -499,15 +494,17 @@
     gin_ref[...] = c32[...].reshape(C, LON, LAT).astype(BF)
     if remote:
         wait(w_all())
-        tiles = [wslab[lax.rem(owner + t, 8), 0] for t in range(8)] + [wslab[owner, 1]]
+        weights = wslab[0].astype(F32)
+        for other in range(1, n_lon):
+            weights = weights + wslab[other].astype(F32)
         wait(k_all())
         small = kslab[0]
         for other in range(1, n_lon):
             small = small + kslab[other]
     else:
-        tiles = [wsend[0, t % 8, 0 if t < 8 else 8].astype(F32) for t in range(PIECES)]
+        weights = wsend[0, 0].astype(F32)
         small = ksend[0, 0]
-    weights = jnp.concatenate(tiles, axis=1) * factor
+    weights = weights * factor
     small = small * factor
     gwin_ref[...] = weights[0:12, 0:HID]
     gwout_ref[0:4, :] = weights[12:16, 0:HID]
@@ -572,20 +569,18 @@
         pltpu.VMEM((C, LAT), F32),
         pltpu.VMEM((C + 16, LAT), F32),
         pltpu.VMEM((16, 16, PACKED), F32),
-        pltpu.VMEM((2, 8, PIECES, 16, LAT), BF),
-        pltpu.VMEM((8, PIECES, 16, LAT), BF),
-        pltpu.VMEM((8, PIECES, 16, LAT), BF),
-        pltpu.VMEM((7, PIECES, 16, LAT), BF),
-        pltpu.VMEM((8, 2, 16, LAT), BF),
-        pltpu.VMEM((7, 2, 16, LAT), BF),
-        pltpu.VMEM((8, 2, 16, LAT), F32),
+        pltpu.VMEM((2, 8, 16, PACKED), BF),
+        pltpu.VMEM((8, 16, PACKED), BF),
+        pltpu.VMEM((8, 16, PACKED), BF),
+        pltpu.VMEM((7, 16, PACKED), BF),
+        pltpu.VMEM((8, 16, PACKED), BF),
         pltpu.VMEM((2, 8, 16, LAT), F32),
         pltpu.VMEM((8, 16, LAT), F32),
         pltpu.VMEM((8, 16, LAT), F32),
         pltpu.VMEM((7, 16, LAT), F32),
         pltpu.VMEM((8, 16, LAT), F32),
-        pltpu.SemaphoreType.DMA((41,)),
-        pltpu.SemaphoreType.DMA((41,)),
+        pltpu.SemaphoreType.DMA((34,)),
+        pltpu.SemaphoreType.DMA((34,)),
     ]
     extra = dict(collective_id=0, has_side_effects=True) if n_lon > 1 else {}
     results = pl.pallas_call(

time: 52 us -> 47.2 us (0.908); the launches traced: 51.9 us -> 46.5 us
  Pallas kernels: 51.2 us -> 45.9 us
    pallas_call x1, Pallas kernels: 48.8 us -> 43.5 us  [block(): pl.pallas_call(functools.partial(kernel_body, n_lon, n_sample, factor), o...]
where the time goes in v4:
time: 47.2 us; the launch traced here: 46.5 us
  Pallas kernels  45.9 us (97%)
  between operations  0.64 us (1%)
    pallas_call x1, Pallas kernels, block(): pl.pallas_call(functools.partial(kernel_body, n_lon, n_sample, factor), o...  43.5 us
    pallas_call x1, Pallas kernels, block(): pl.pallas_call(deliver, out_shape=outs, in_specs=[anywhere] * 6, out_spec...  2.4 us

profile of v4, /device:TPU:0, one launch (start us, length us, event | category | flops | bytes accessed | tf_op | source)
XLA Modules:
  0.0 46.5 jit_solution(4785567183505260326)
XLA Ops:
  0.6 43.5 %shard_map.172 = (bf16[192,16,128]{2,1,0:T(8,128)(2,1)}, bf16[192,16,128]{2,1,0:T(8,128)(2,1)}, f32[12,768]{1,0:T(8,128)}, f32[12,768]{1,0:T(8,128)}, f32[7,7,12]{2,1,0:T(8,128)}, /*index=5*/f32[1,12]{1,0:T(1,128)}) custom-call(bf16[192,16,128]{2,1,0:T(8,128)(2,1)} %bitcast.10, bf16[192,16,128]{2,1,0:T(8,128)(2,1)} %bitcast.11, s32[16,128]{1,0:T(8,128)} %sea_ref.1, ...), custom_call_target="tpu_custom_call" | custom-call | tf_op jit(solution)/shard_map/pallas_call | solution.py:586
  44.1 2.4 %shard_map.173 = (bf16[192,16,128]{2,1,0:T(8,128)(2,1)}, bf16[192,16,128]{2,1,0:T(8,128)(2,1)}, f32[12,768]{1,0:T(8,128)}, f32[12,768]{1,0:T(8,128)}, f32[7,7,12]{2,1,0:T(8,128)}, /*index=5*/f32[1,12]{1,0:T(1,128)}) custom-call(bf16[192,16,128]{2,1,0:T(8,128)(2,1)} %get-tuple-element.18.refs_0_, bf16[192,16,128]{2,1,0:T(8,128)(2,1)} %get-tuple-element.19.refs_1_, ...), custom_call_target="tpu_custom_call" | custom-call | tf_op jit(solution)/shard_map/pallas_call | solution.py:604

commit v5 on v4

--- a/solution.py
+++ b/solution.py
@@ -88,11 +88,11 @@
     gather = np.zeros((SPEC, LAT))
     gather[:, :8] = taps.T
     return (
+        spread,
         stacked(field_f),
+        beside(back_f),
         np.concatenate([stacked(back_f.T), stacked(field_b)], axis=1),
-        beside(back_f),
         beside(back_b),
-        spread,
         beside(gather),
     )
 
@@ -106,24 +106,33 @@
     n_sample,
     factor,
     state_ref,
-    cot_ref,
     sea_ref,
     taps_ref,
     gain_ref,
-    win_ref,
-    wout_t,
-    field_f,
-    field_g,
-    back_f,
-    back_b,
-    spread,
-    gather,
+    cot_far,
+    win_far,
+    wout_far,
+    spread_far,
+    field_f_far,
+    back_f_far,
+    field_g_far,
+    back_b_far,
+    gather_far,
     sout_ref,
     gin_ref,
     gwin_ref,
     gwout_ref,
     gk_ref,
     gg_ref,
+    cot_ref,
+    win_ref,
+    wout_t,
+    spread,
+    field_f,
+    back_f,
+    field_g,
+    back_b,
+    gather,
     x32,
     c32,
     xa,
@@ -160,9 +169,29 @@
     kmid,
     kparts,
     kslab,
+    kout,
     send,
     recv,
+    near,
 ):
+    fetches = [
+        pltpu.make_async_copy(far, here, near.at[k])
+        for k, (far, here) in enumerate(
+            (
+                (spread_far, spread),
+                (field_f_far, field_f),
+                (back_f_far, back_f),
+                (win_far, win_ref),
+                (wout_far, wout_t),
+                (cot_far, cot_ref),
+                (field_g_far, field_g),
+                (back_b_far, back_b),
+                (gather_far, gather),
+            )
+        )
+    ]
+    for fetch in fetches:
+        fetch.start()
     remote = n_lon > 1
     if remote:
         lon = lax.axis_index("lon")
@@ -205,17 +234,17 @@
         ref[LON + HALO : LON + 2 * HALO] = ref[HALO : 2 * HALO]
 
     x32[...] = state_ref[...].astype(F32).reshape(C * LON, LAT)
-    for i in (13, 14, 15, 0, 1, 2):
-        own = column(x32, i)
-        xa[HALO + i] = own.astype(BF)
+    for i in (0, 1, 2, 13, 14, 15):
+        xa[HALO + i] = column(x32, i).astype(BF)
     if remote:
         pl.semaphore_wait(barrier, len(peers))
-        x_halo = halo_copies(xa, 0)
-        for one in x_halo:
-            one.start()
+        x_right, x_left = halo_copies(xa, 0)
+        x_left.start()
+        x_right.start()
     for i in range(3, 13):
-        own = column(x32, i)
-        xa[HALO + i] = own.astype(BF)
+        xa[HALO + i] = column(x32, i).astype(BF)
+    for fetch in fetches:
+        fetch.wait()
     c32[...] = cot_ref[...].astype(F32).reshape(C * LON, LAT)
 
     flat_taps[...] = jnp.zeros_like(flat_taps)
@@ -263,7 +292,7 @@
                 ).astype(BF)
             return carry
 
-        lax.fori_loop(0, C // TILE, one_tile, 0)
+        lax.fori_loop(0, C // TILE, one_tile, 0, unroll=2)
         main = matmul(sum_high[...].reshape(GROUP * C, SPEC), inverse[...])
         rest = matmul(sum_low[...].reshape(GROUP * C, SPEC), inverse[:, 0:LAT])
         return (main[:, 0:LAT] + main[:, LAT:] + rest).reshape(GROUP, C, LAT)
@@ -334,10 +363,6 @@
             gw[col + k] = spectrum[:, 0:SPEC]
             gh[HALO + col + k] = spectrum[:, SPEC:]
 
-    def fill_halo():
-        field_spectrum(0, HALO)
-        field_spectrum(LON + HALO, HALO)
-
     def in_groups(first, last, work):
         def one_group(step, carry):
             work(lax.rem(GROUP + step * GROUP, LON))
@@ -370,7 +395,7 @@
                     dkf[pl.ds(at, 8), spot] = total
             return carry
 
-        lax.fori_loop(0, C // 8, one_tile, 0)
+        lax.fori_loop(0, C // 8, one_tile, 0, unroll=2)
 
     in_groups(0, 2, forward_group)
     in_groups(0, 2, backward_mlp)
@@ -379,11 +404,21 @@
     acc_out[...] = matmul_nt(cot_all[:, cells], hid_all[:, cells])
     acc_in[...] = matmul_nt(norm_all[:, cells], gp_all[:, cells])
     if remote:
-        wait(x_halo)
+        g_right, g_left = halo_copies(ga, 2)
+        x_left.wait()
     else:
         local_halo(xa)
-    fill_halo()
-    in_groups(2, 4, forward_group)
+    field_spectrum(LON + HALO, HALO)
+    forward_group(LON - GROUP)
+    backward_mlp(LON - GROUP)
+    if remote:
+        g_right.start()
+        x_right.wait()
+    field_spectrum(0, HALO)
+    forward_group(0)
+    backward_mlp(0)
+    if remote:
+        g_left.start()
 
     for cells in (slice(0, GROUP * LAT), slice(3 * GROUP * LAT, LON * LAT)):
         acc_out[...] += matmul_nt(cot_all[:, cells], hid_all[:, cells])
@@ -431,14 +466,11 @@
             return to_slabs(kslab, 27)
 
         start(w_core())
-    in_groups(2, 4, backward_mlp)
-    if remote:
-        g_halo = halo_copies(ga, 2)
-        start(g_halo)
+    filter_grads([(0, GROUP), (3 * GROUP, GROUP)], False)
+    if remote:
         wait(w_core())
         wmid[...] = (wsend[core].astype(F32) + wcore[...].astype(F32)).astype(BF)
         start(w_own())
-    filter_grads([(0, GROUP), (3 * GROUP, GROUP)], False)
 
     lanes = lax.broadcasted_iota(jnp.int32, (C, LAT), 1)
     total = jnp.where(lanes == TAPS * TAPS, jnp.sum(acc_gain[...], axis=1, keepdims=True), 0.0)
@@ -449,10 +481,13 @@
         both = matmul(high, gather[...])
         found = both[:, 0:LAT] + both[:, LAT:] + matmul(low, gather[:, 0:LAT])
         total = total + (pltpu.roll(found, a * TAPS, axis=1) if a else found)
-    dks[0:C, :] = total
-    dks[C : C + 16, :] = jnp.zeros((16, LAT), F32)
+    dks[0, 0:C, :] = total
+    dks[1, 0:C, :] = pltpu.roll(total, LAT // 2, axis=1)
+    for side in range(2):
+        dks[side, C : C + 16, :] = jnp.zeros((16, LAT), F32)
     for o in range(16):
-        ksend[o % 2, o // 2] = dks[OWN * o : OWN * o + 16, :]
+        at = OWN * o
+        ksend[o % 2, o // 2] = dks[0, at : at + 8, :] + dks[1, at + 6 : at + 14, :]
     if remote:
         start(k_core())
     in_groups(0, 4, finish_state)
@@ -470,26 +505,27 @@
 
     in_groups(0, 2, backward_group)
     if remote:
+        g_right.wait()
+    else:
+        local_halo(ga)
+    grad_spectrum(0, HALO)
+    backward_group(0)
+    if remote:
         wait(w_own())
         held = wmid[owner].astype(F32)
         for d in range(len(owners)):
             held = held + wparts[d].astype(F32)
         wslab[lon] = held.astype(BF)
         start(w_all())
-        wait(g_halo)
-    else:
-        local_halo(ga)
-    grad_spectrum(0, HALO)
-    grad_spectrum(LON + HALO, HALO)
-    in_groups(2, 3, backward_group)
-    if remote:
         wait(k_own())
         held = kmid[owner]
         for d in range(len(owners)):
             held = held + kparts[d]
         kslab[lon] = held
         start(k_all())
-    in_groups(3, 4, backward_group)
+        g_left.wait()
+    grad_spectrum(LON + HALO, HALO)
+    backward_group(LON - GROUP)
     sout_ref[...] = x32[...].reshape(C, LON, LAT).astype(BF)
     gin_ref[...] = c32[...].reshape(C, LON, LAT).astype(BF)
     if remote:
@@ -510,7 +546,9 @@
     gwout_ref[0:4, :] = weights[12:16, 0:HID]
     gwout_ref[4:12, 0:wide] = weights[0:8, HID:PACKED]
     gwout_ref[4:12, wide:HID] = weights[8:16, HID:PACKED]
-    small_t = small.T
+    kout[0:6, :] = small[0:6, :]
+    kout[6:12, :] = pltpu.roll(small, LAT // 2, axis=1)[0:6, :]
+    small_t = kout[...].T
     for a in range(TAPS):
         gk_ref[a] = small_t[a * TAPS : (a + 1) * TAPS, 0:OWN]
     gg_ref[...] = small_t[TAPS * TAPS : TAPS * TAPS + 1, 0:OWN]
@@ -533,6 +571,7 @@
 
 def block(n_lon, n_sample, factor, state, cot, sea, taps, gain, win, wout):
     vmem = pl.BlockSpec(memory_space=pltpu.VMEM)
+    far = pl.BlockSpec(memory_space=pltpu.HBM)
     shape = jax.ShapeDtypeStruct
     outs = (
         shape((C, LON, LAT), BF),
@@ -543,6 +582,15 @@
         shape((1, OWN), F32),
     )
     scratch = [
+        pltpu.VMEM((C, LON, LAT), BF),
+        pltpu.VMEM((C, HID), BF),
+        pltpu.VMEM((C, HID), BF),
+        pltpu.VMEM((3 * 64, TAPS * SPEC), BF),
+        pltpu.VMEM((2 * LAT, SPEC), BF),
+        pltpu.VMEM((SPEC, 2 * LAT), BF),
+        pltpu.VMEM((2 * LAT, 2 * SPEC), BF),
+        pltpu.VMEM((SPEC, 2 * LAT), BF),
+        pltpu.VMEM((SPEC, 2 * LAT), BF),
         pltpu.VMEM((C * LON, LAT), F32),
         pltpu.VMEM((C * LON, LAT), F32),
         pltpu.VMEM((LON + 2 * HALO, C, LAT), BF),
@@ -567,35 +615,37 @@
         pltpu.VMEM((C, HID), F32),
         pltpu.VMEM((C, HID), F32),
         pltpu.VMEM((C, LAT), F32),
-        pltpu.VMEM((C + 16, LAT), F32),
+        pltpu.VMEM((2, C + 16, LAT), F32),
         pltpu.VMEM((16, 16, PACKED), F32),
         pltpu.VMEM((2, 8, 16, PACKED), BF),
         pltpu.VMEM((8, 16, PACKED), BF),
         pltpu.VMEM((8, 16, PACKED), BF),
         pltpu.VMEM((7, 16, PACKED), BF),
         pltpu.VMEM((8, 16, PACKED), BF),
-        pltpu.VMEM((2, 8, 16, LAT), F32),
-        pltpu.VMEM((8, 16, LAT), F32),
-        pltpu.VMEM((8, 16, LAT), F32),
-        pltpu.VMEM((7, 16, LAT), F32),
-        pltpu.VMEM((8, 16, LAT), F32),
+        pltpu.VMEM((2, 8, 8, LAT), F32),
+        pltpu.VMEM((8, 8, LAT), F32),
+        pltpu.VMEM((8, 8, LAT), F32),
+        pltpu.VMEM((7, 8, LAT), F32),
+        pltpu.VMEM((8, 8, LAT), F32),
+        pltpu.VMEM((16, LAT), F32),
         pltpu.SemaphoreType.DMA((34,)),
         pltpu.SemaphoreType.DMA((34,)),
+        pltpu.SemaphoreType.DMA((9,)),
     ]
     extra = dict(collective_id=0, has_side_effects=True) if n_lon > 1 else {}
     results = pl.pallas_call(
         functools.partial(kernel_body, n_lon, n_sample, factor),
         out_shape=outs,
-        in_specs=[vmem] * 13,
+        in_specs=[vmem] * 4 + [far] * 9,
         out_specs=(vmem,) * 6,
         scratch_shapes=scratch,
-        compiler_params=pltpu.CompilerParams(vmem_limit_bytes=60 * 1024 * 1024, **extra),
+        compiler_params=pltpu.CompilerParams(vmem_limit_bytes=62 * 1024 * 1024, **extra),
     )(
         state.reshape(C, LON, LAT),
-        cot.reshape(C, LON, LAT),
         sea,
         taps.transpose(1, 2, 0),
         gain.reshape(1, C),
+        cot.reshape(C, LON, LAT),
         win,
         wout.T,
         *spectral_constants(),

time: 47.2 us -> 43.4 us (0.919)
  Pallas kernels: 45.9 us -> 42.2 us
    pallas_call x1, Pallas kernels: 43.5 us -> 39.8 us  [block(): pl.pallas_call(functools.partial(kernel_body, n_lon, n_sample, factor), o...]
where the time goes in v5:
time: 43.4 us; the launch traced here: 42.8 us
  Pallas kernels  42.2 us (97%)
  between operations  0.64 us (1%)
    pallas_call x1, Pallas kernels, block(): pl.pallas_call(functools.partial(kernel_body, n_lon, n_sample, factor), o...  39.8 us
    pallas_call x1, Pallas kernels, block(): pl.pallas_call(deliver, out_shape=outs, in_specs=[anywhere] * 6, out_spec...  2.4 us

profile of v5, /device:TPU:0, one launch (start us, length us, event | category | flops | bytes accessed | tf_op | source)
XLA Modules:
  0.0 42.8 jit_solution(6782639437324856573)
XLA Ops:
  0.6 39.8 %shard_map.172 = (bf16[192,16,128]{2,1,0:T(8,128)(2,1)}, bf16[192,16,128]{2,1,0:T(8,128)(2,1)}, f32[12,768]{1,0:T(8,128)}, f32[12,768]{1,0:T(8,128)}, f32[7,7,12]{2,1,0:T(8,128)}, /*index=5*/f32[1,12]{1,0:T(1,128)}) custom-call(bf16[192,16,128]{2,1,0:T(8,128)(2,1)} %bitcast.10, s32[16,128]{1,0:T(8,128)} %sea_ref.1, f32[7,7,192]{2,1,0:T(8,128)} %bitcast.13, ...), custom_call_target="tpu_custom_call" | custom-call | tf_op jit(solution)/shard_map/pallas_call | solution.py:636
  40.4 2.4 %shard_map.173 = (bf16[192,16,128]{2,1,0:T(8,128)(2,1)}, bf16[192,16,128]{2,1,0:T(8,128)(2,1)}, f32[12,768]{1,0:T(8,128)}, f32[12,768]{1,0:T(8,128)}, f32[7,7,12]{2,1,0:T(8,128)}, /*index=5*/f32[1,12]{1,0:T(1,128)}) custom-call(bf16[192,16,128]{2,1,0:T(8,128)(2,1)} %get-tuple-element.18.refs_0_, bf16[192,16,128]{2,1,0:T(8,128)(2,1)} %get-tuple-element.19.refs_1_, ...), custom_call_target="tpu_custom_call" | custom-call | tf_op jit(solution)/shard_map/pallas_call | solution.py:654

commit v6 on v5

--- a/solution.py
+++ b/solution.py
@@ -23,6 +23,7 @@
 TILE = 16
 OWN = 12
 PACKED = 1152
+PIECES = PACKED // LAT
 BF = jnp.bfloat16
 F32 = jnp.float32
 MESH = pl.DeviceIdType.MESH
@@ -163,6 +164,8 @@
     wcore,
     wmid,
     wparts,
+    bsend,
+    bparts,
     wslab,
     ksend,
     kcore,
@@ -190,8 +193,6 @@
             )
         )
     ]
-    for fetch in fetches:
-        fetch.start()
     remote = n_lon > 1
     if remote:
         lon = lax.axis_index("lon")
@@ -241,6 +242,8 @@
         x_right, x_left = halo_copies(xa, 0)
         x_left.start()
         x_right.start()
+    for fetch in fetches:
+        fetch.start()
     for i in range(3, 13):
         xa[HALO + i] = column(x32, i).astype(BF)
     for fetch in fetches:
@@ -410,15 +413,10 @@
         local_halo(xa)
     field_spectrum(LON + HALO, HALO)
     forward_group(LON - GROUP)
-    backward_mlp(LON - GROUP)
-    if remote:
-        g_right.start()
+    if remote:
         x_right.wait()
     field_spectrum(0, HALO)
     forward_group(0)
-    backward_mlp(0)
-    if remote:
-        g_left.start()
 
     for cells in (slice(0, GROUP * LAT), slice(3 * GROUP * LAT, LON * LAT)):
         acc_out[...] += matmul_nt(cot_all[:, cells], hid_all[:, cells])
@@ -431,7 +429,10 @@
         stage[o, 0:8, HID:PACKED] = acc_out[at + 4 : at + 12, 0:wide]
         stage[o, 8:16, HID:PACKED] = acc_out[at + 4 : at + 12, wide:HID]
     for o in range(16):
-        wsend[o % 2, o // 2] = stage[o].astype(BF)
+        q = o // 2
+        for t in range(PIECES):
+            slot = q if t < 8 else 8
+            wsend[o % 2, (q + t) % 8, slot] = stage[o, :, t * LAT : (t + 1) * LAT].astype(BF)
 
     if remote:
 
@@ -450,27 +451,38 @@
         def w_core():
             return [copy(wsend.at[1 - core], wcore, 4, partner)]
 
+        def w_lon():
+            return [
+                copy(wmid.at[other], wparts.at[d], 5 + d, {"lon": other})
+                for d, other in enumerate(slabs)
+            ]
+
         def w_own():
-            return to_owners(wmid, wparts, 5)
+            return to_owners(bsend, bparts, 12)
 
         def w_all():
-            return to_slabs(wslab, 12)
+            return to_slabs(wslab, 19)
 
         def k_core():
-            return [copy(ksend.at[1 - core], kcore, 19, partner)]
+            return [copy(ksend.at[1 - core], kcore, 26, partner)]
 
         def k_own():
-            return to_owners(kmid, kparts, 20)
+            return to_owners(kmid, kparts, 27)
 
         def k_all():
-            return to_slabs(kslab, 27)
+            return to_slabs(kslab, 34)
 
         start(w_core())
-    filter_grads([(0, GROUP), (3 * GROUP, GROUP)], False)
+    backward_mlp(LON - GROUP)
+    if remote:
+        g_right.start()
+    backward_mlp(0)
     if remote:
         wait(w_core())
         wmid[...] = (wsend[core].astype(F32) + wcore[...].astype(F32)).astype(BF)
-        start(w_own())
+        start(w_lon())
+        g_left.start()
+    filter_grads([(0, GROUP), (3 * GROUP, GROUP)], False)
 
     lanes = lax.broadcasted_iota(jnp.int32, (C, LAT), 1)
     total = jnp.where(lanes == TAPS * TAPS, jnp.sum(acc_gain[...], axis=1, keepdims=True), 0.0)
@@ -490,11 +502,12 @@
         ksend[o % 2, o // 2] = dks[0, at : at + 8, :] + dks[1, at + 6 : at + 14, :]
     if remote:
         start(k_core())
-    in_groups(0, 4, finish_state)
+    in_groups(0, 2, finish_state)
     if remote:
         wait(k_core())
         kmid[...] = ksend[core] + kcore[...]
         start(k_own())
+    in_groups(2, 4, finish_state)
 
     def backward_group(col):
         moved = filtered(gh, col, True, back_b)
@@ -503,7 +516,18 @@
             at = pl.ds(col + k, C, stride=LON)
             c32[at, :] = c32[at, :] * mask[k] + moved[k]
 
-    in_groups(0, 2, backward_group)
+    in_groups(0, 1, backward_group)
+    if remote:
+        wait(w_lon())
+        total = wmid[lon].astype(F32)
+        for d in range(len(slabs)):
+            total = total + wparts[d].astype(F32)
+        total = total.astype(BF)
+        for q in range(8):
+            bsend[q, 0] = total[q]
+            bsend[q, 1] = total[8]
+        start(w_own())
+    in_groups(1, 2, backward_group)
     if remote:
         g_right.wait()
     else:
@@ -511,12 +535,6 @@
     grad_spectrum(0, HALO)
     backward_group(0)
     if remote:
-        wait(w_own())
-        held = wmid[owner].astype(F32)
-        for d in range(len(owners)):
-            held = held + wparts[d].astype(F32)
-        wslab[lon] = held.astype(BF)
-        start(w_all())
         wait(k_own())
         held = kmid[owner]
         for d in range(len(owners)):
@@ -526,20 +544,26 @@
         g_left.wait()
     grad_spectrum(LON + HALO, HALO)
     backward_group(LON - GROUP)
+    if remote:
+        wait(w_own())
+        held = bsend[owner].astype(F32)
+        for d in range(len(owners)):
+            held = held + bparts[d].astype(F32)
+        wslab[lon] = held.astype(BF)
+        start(w_all())
     sout_ref[...] = x32[...].reshape(C, LON, LAT).astype(BF)
     gin_ref[...] = c32[...].reshape(C, LON, LAT).astype(BF)
     if remote:
-        wait(w_all())
-        weights = wslab[0].astype(F32)
-        for other in range(1, n_lon):
-            weights = weights + wslab[other].astype(F32)
         wait(k_all())
         small = kslab[0]
         for other in range(1, n_lon):
             small = small + kslab[other]
+        wait(w_all())
+        tiles = [wslab[lax.rem(owner + t, 8), 0] for t in range(8)] + [wslab[owner, 1]]
     else:
-        weights = wsend[0, 0].astype(F32)
+        tiles = [wsend[0, t % 8, 0 if t < 8 else 8] for t in range(PIECES)]
         small = ksend[0, 0]
+    weights = jnp.concatenate(tiles, axis=1).astype(F32)
     weights = weights * factor
     small = small * factor
     gwin_ref[...] = weights[0:12, 0:HID]
@@ -617,19 +641,21 @@
         pltpu.VMEM((C, LAT), F32),
         pltpu.VMEM((2, C + 16, LAT), F32),
         pltpu.VMEM((16, 16, PACKED), F32),
-        pltpu.VMEM((2, 8, 16, PACKED), BF),
-        pltpu.VMEM((8, 16, PACKED), BF),
-        pltpu.VMEM((8, 16, PACKED), BF),
-        pltpu.VMEM((7, 16, PACKED), BF),
-        pltpu.VMEM((8, 16, PACKED), BF),
+        pltpu.VMEM((2, 8, PIECES, 16, LAT), BF),
+        pltpu.VMEM((8, PIECES, 16, LAT), BF),
+        pltpu.VMEM((8, PIECES, 16, LAT), BF),
+        pltpu.VMEM((7, PIECES, 16, LAT), BF),
+        pltpu.VMEM((8, 2, 16, LAT), BF),
+        pltpu.VMEM((7, 2, 16, LAT), BF),
+        pltpu.VMEM((8, 2, 16, LAT), BF),
         pltpu.VMEM((2, 8, 8, LAT), F32),
         pltpu.VMEM((8, 8, LAT), F32),
         pltpu.VMEM((8, 8, LAT), F32),
         pltpu.VMEM((7, 8, LAT), F32),
         pltpu.VMEM((8, 8, LAT), F32),
         pltpu.VMEM((16, LAT), F32),
-        pltpu.SemaphoreType.DMA((34,)),
-        pltpu.SemaphoreType.DMA((34,)),
+        pltpu.SemaphoreType.DMA((41,)),
+        pltpu.SemaphoreType.DMA((41,)),
         pltpu.SemaphoreType.DMA((9,)),
     ]
     extra = dict(collective_id=0, has_side_effects=True) if n_lon > 1 else {}

time: 43.4 us -> 49.4 us (1.14)
  Pallas kernels: 42.2 us -> 48.5 us
    pallas_call x1, Pallas kernels: 39.8 us -> 46.1 us  [block(): pl.pallas_call(functools.partial(kernel_body, n_lon, n_sample, factor), o...]
where the time goes in v6:
time: 49.4 us; the launch traced here: 49.2 us
  Pallas kernels  48.5 us (98%)
  between operations  0.64 us (1%)
    pallas_call x1, Pallas kernels, block(): pl.pallas_call(functools.partial(kernel_body, n_lon, n_sample, factor), o...  46.1 us
    pallas_call x1, Pallas kernels, block(): pl.pallas_call(deliver, out_shape=outs, in_specs=[anywhere] * 6, out_spec...  2.4 us

profile of v6, /device:TPU:0, one launch (start us, length us, event | category | flops | bytes accessed | tf_op | source)
XLA Modules:
  0.0 49.2 jit_solution(5341494079611590536)
XLA Ops:
  0.6 46.1 %shard_map.172 = (bf16[192,16,128]{2,1,0:T(8,128)(2,1)}, bf16[192,16,128]{2,1,0:T(8,128)(2,1)}, f32[12,768]{1,0:T(8,128)}, f32[12,768]{1,0:T(8,128)}, f32[7,7,12]{2,1,0:T(8,128)}, /*index=5*/f32[1,12]{1,0:T(1,128)}) custom-call(bf16[192,16,128]{2,1,0:T(8,128)(2,1)} %bitcast.10, s32[16,128]{1,0:T(8,128)} %sea_ref.1, f32[7,7,192]{2,1,0:T(8,128)} %bitcast.13, ...), custom_call_target="tpu_custom_call" | custom-call | tf_op jit(solution)/shard_map/pallas_call | solution.py:662
  46.8 2.4 %shard_map.173 = (bf16[192,16,128]{2,1,0:T(8,128)(2,1)}, bf16[192,16,128]{2,1,0:T(8,128)(2,1)}, f32[12,768]{1,0:T(8,128)}, f32[12,768]{1,0:T(8,128)}, f32[7,7,12]{2,1,0:T(8,128)}, /*index=5*/f32[1,12]{1,0:T(1,128)}) custom-call(bf16[192,16,128]{2,1,0:T(8,128)(2,1)} %get-tuple-element.18.refs_0_, bf16[192,16,128]{2,1,0:T(8,128)(2,1)} %get-tuple-element.19.refs_1_, ...), custom_call_target="tpu_custom_call" | custom-call | tf_op jit(solution)/shard_map/pallas_call | solution.py:680

commit v7 on v5

--- a/solution.py
+++ b/solution.py
@@ -19,6 +19,7 @@
 HALO = 3
 GROUP = 4
 HID_BLOCK = 256
+CUTS = 4
 CELL_BLOCK = 256
 TILE = 16
 OWN = 12
@@ -164,9 +165,14 @@
     wmid,
     wparts,
     wslab,
+    vsend,
+    vcore,
+    vmid,
+    vparts,
+    vslab,
+    sout_buf,
+    gin_buf,
     ksend,
-    kcore,
-    kmid,
     kparts,
     kslab,
     kout,
@@ -190,8 +196,6 @@
             )
         )
     ]
-    for fetch in fetches:
-        fetch.start()
     remote = n_lon > 1
     if remote:
         lon = lax.axis_index("lon")
@@ -204,9 +208,11 @@
         left = {"lon": lax.rem(lon + n_lon - 1, n_lon)}
         owners = [lax.rem(owner + d, n_own) for d in range(1, n_own)]
         slabs = [lax.rem(lon + d, n_lon) for d in range(1, n_lon)]
+        samples = [lax.rem(sample + d, n_sample) for d in range(1, n_sample)]
         peers = (
             [partner]
             + [{"sample": 2 * other + core} for other in owners]
+            + [{"sample": 2 * other + 1 - core} for other in owners]
             + [{"lon": other} for other in slabs]
         )
         barrier = pltpu.get_barrier_semaphore()
@@ -241,6 +247,8 @@
         x_right, x_left = halo_copies(xa, 0)
         x_left.start()
         x_right.start()
+    for fetch in fetches:
+        fetch.start()
     for i in range(3, 13):
         xa[HALO + i] = column(x32, i).astype(BF)
     for fetch in fetches:
@@ -431,7 +439,8 @@
         stage[o, 0:8, HID:PACKED] = acc_out[at + 4 : at + 12, 0:wide]
         stage[o, 8:16, HID:PACKED] = acc_out[at + 4 : at + 12, wide:HID]
     for o in range(16):
-        wsend[o % 2, o // 2] = stage[o].astype(BF)
+        wsend[o % 2, o // 2] = stage[o, :, 0:HID].astype(BF)
+        vsend[o % 2, o // 2] = stage[o, :, HID:PACKED].astype(BF)
 
     if remote:
 
@@ -441,36 +450,33 @@
                 for d, other in enumerate(slabs)
             ]
 
+        def to_core(packed, from_core, base):
+            return [copy(packed.at[1 - core], from_core, base, partner)]
+
         def to_owners(source, target, base):
             return [
                 copy(source.at[other], target.at[d], base + d, {"sample": 2 * other + core})
                 for d, other in enumerate(owners)
             ]
 
-        def w_core():
-            return [copy(wsend.at[1 - core], wcore, 4, partner)]
-
-        def w_own():
-            return to_owners(wmid, wparts, 5)
-
-        def w_all():
-            return to_slabs(wslab, 12)
-
-        def k_core():
-            return [copy(ksend.at[1 - core], kcore, 19, partner)]
-
         def k_own():
-            return to_owners(kmid, kparts, 20)
+            return [
+                copy(ksend.at[other], kparts.at[d], 34 + d, {"sample": other})
+                for d, other in enumerate(samples)
+            ]
 
         def k_all():
-            return to_slabs(kslab, 27)
-
-        start(w_core())
+            return to_slabs(kslab, 49)
+
+        halves = ((wsend, wcore, wmid, wparts, wslab, 4), (vsend, vcore, vmid, vparts, vslab, 19))
+        for packed, from_core, _, _, _, base in halves:
+            start(to_core(packed, from_core, base))
     filter_grads([(0, GROUP), (3 * GROUP, GROUP)], False)
     if remote:
-        wait(w_core())
-        wmid[...] = (wsend[core].astype(F32) + wcore[...].astype(F32)).astype(BF)
-        start(w_own())
+        for packed, from_core, middle, parts, _, base in halves:
+            wait(to_core(packed, from_core, base))
+            middle[...] = (packed[core].astype(F32) + from_core[...].astype(F32)).astype(BF)
+            start(to_owners(middle, parts, base + 1))
 
     lanes = lax.broadcasted_iota(jnp.int32, (C, LAT), 1)
     total = jnp.where(lanes == TAPS * TAPS, jnp.sum(acc_gain[...], axis=1, keepdims=True), 0.0)
@@ -487,14 +493,10 @@
         dks[side, C : C + 16, :] = jnp.zeros((16, LAT), F32)
     for o in range(16):
         at = OWN * o
-        ksend[o % 2, o // 2] = dks[0, at : at + 8, :] + dks[1, at + 6 : at + 14, :]
-    if remote:
-        start(k_core())
+        ksend[o] = dks[0, at : at + 8, :] + dks[1, at + 6 : at + 14, :]
+    if remote:
+        start(k_own())
     in_groups(0, 4, finish_state)
-    if remote:
-        wait(k_core())
-        kmid[...] = ksend[core] + kcore[...]
-        start(k_own())
 
     def backward_group(col):
         moved = filtered(gh, col, True, back_b)
@@ -510,36 +512,48 @@
         local_halo(ga)
     grad_spectrum(0, HALO)
     backward_group(0)
-    if remote:
-        wait(w_own())
-        held = wmid[owner].astype(F32)
-        for d in range(len(owners)):
-            held = held + wparts[d].astype(F32)
-        wslab[lon] = held.astype(BF)
-        start(w_all())
+    sout_buf[...] = x32[...].reshape(C, LON, LAT).astype(BF)
+    leave = [
+        pltpu.make_async_copy(sout_buf, sout_ref, near.at[9]),
+        pltpu.make_async_copy(gin_buf, gin_ref, near.at[10]),
+    ]
+    leave[0].start()
+    if remote:
+        g_left.wait()
+    grad_spectrum(LON + HALO, HALO)
+    backward_group(LON - GROUP)
+    if remote:
         wait(k_own())
-        held = kmid[owner]
-        for d in range(len(owners)):
+        held = ksend[sample]
+        for d in range(len(samples)):
             held = held + kparts[d]
         kslab[lon] = held
         start(k_all())
-        g_left.wait()
-    grad_spectrum(LON + HALO, HALO)
-    backward_group(LON - GROUP)
-    sout_ref[...] = x32[...].reshape(C, LON, LAT).astype(BF)
-    gin_ref[...] = c32[...].reshape(C, LON, LAT).astype(BF)
-    if remote:
-        wait(w_all())
-        weights = wslab[0].astype(F32)
-        for other in range(1, n_lon):
-            weights = weights + wslab[other].astype(F32)
+    gin_buf[...] = c32[...].reshape(C, LON, LAT).astype(BF)
+    leave[1].start()
+    if remote:
+        for _, _, middle, parts, slab, base in halves:
+            wait(to_owners(middle, parts, base + 1))
+            held = middle[owner].astype(F32)
+            for d in range(len(owners)):
+                held = held + parts[d].astype(F32)
+            slab[lon] = held.astype(BF)
+            start(to_slabs(slab, base + 8))
         wait(k_all())
         small = kslab[0]
         for other in range(1, n_lon):
             small = small + kslab[other]
+        sums = []
+        for _, _, _, _, slab, base in halves:
+            wait(to_slabs(slab, base + 8))
+            held = slab[0].astype(F32)
+            for other in range(1, n_lon):
+                held = held + slab[other].astype(F32)
+            sums.append(held)
+        weights = jnp.concatenate(sums, axis=1)
     else:
-        weights = wsend[0, 0].astype(F32)
-        small = ksend[0, 0]
+        weights = jnp.concatenate([wsend[0, 0], vsend[0, 0]], axis=1).astype(F32)
+        small = ksend[0]
     weights = weights * factor
     small = small * factor
     gwin_ref[...] = weights[0:12, 0:HID]
@@ -552,19 +566,28 @@
     for a in range(TAPS):
         gk_ref[a] = small_t[a * TAPS : (a + 1) * TAPS, 0:OWN]
     gg_ref[...] = small_t[TAPS * TAPS : TAPS * TAPS + 1, 0:OWN]
+    for one in leave:
+        one.wait()
 
 
 def deliver(*refs):
     count = len(refs) // 3
     sems = refs[-1]
-    sources, targets, held = refs[:count], refs[count : 2 * count], refs[2 * count : 3 * count]
-    arrive = [pltpu.make_async_copy(sources[k], held[k], sems.at[0, k]) for k in range(count)]
-    leave = [pltpu.make_async_copy(held[k], targets[k], sems.at[1, k]) for k in range(count)]
+    arrive, leave = [], []
+    for k in range(count):
+        source, target, held = refs[k], refs[count + k], refs[2 * count + k]
+        pieces = CUTS if k < 2 else 1
+        length = source.shape[0] // pieces
+        for p in range(pieces):
+            part = pl.ds(p * length, length)
+            at = len(arrive)
+            arrive.append(pltpu.make_async_copy(source.at[part], held.at[part], sems.at[0, at]))
+            leave.append(pltpu.make_async_copy(held.at[part], target.at[part], sems.at[1, at]))
     for one in arrive:
         one.start()
-    for k in range(count):
-        arrive[k].wait()
-        leave[k].start()
+    for one, other in zip(arrive, leave):
+        one.wait()
+        other.start()
     for one in leave:
         one.wait()
 
@@ -617,27 +640,32 @@
         pltpu.VMEM((C, LAT), F32),
         pltpu.VMEM((2, C + 16, LAT), F32),
         pltpu.VMEM((16, 16, PACKED), F32),
-        pltpu.VMEM((2, 8, 16, PACKED), BF),
-        pltpu.VMEM((8, 16, PACKED), BF),
-        pltpu.VMEM((8, 16, PACKED), BF),
-        pltpu.VMEM((7, 16, PACKED), BF),
-        pltpu.VMEM((8, 16, PACKED), BF),
-        pltpu.VMEM((2, 8, 8, LAT), F32),
-        pltpu.VMEM((8, 8, LAT), F32),
-        pltpu.VMEM((8, 8, LAT), F32),
-        pltpu.VMEM((7, 8, LAT), F32),
+        pltpu.VMEM((2, 8, 16, HID), BF),
+        pltpu.VMEM((8, 16, HID), BF),
+        pltpu.VMEM((8, 16, HID), BF),
+        pltpu.VMEM((7, 16, HID), BF),
+        pltpu.VMEM((8, 16, HID), BF),
+        pltpu.VMEM((2, 8, 16, HID // 2), BF),
+        pltpu.VMEM((8, 16, HID // 2), BF),
+        pltpu.VMEM((8, 16, HID // 2), BF),
+        pltpu.VMEM((7, 16, HID // 2), BF),
+        pltpu.VMEM((8, 16, HID // 2), BF),
+        pltpu.VMEM((C, LON, LAT), BF),
+        pltpu.VMEM((C, LON, LAT), BF),
+        pltpu.VMEM((16, 8, LAT), F32),
+        pltpu.VMEM((15, 8, LAT), F32),
         pltpu.VMEM((8, 8, LAT), F32),
         pltpu.VMEM((16, LAT), F32),
-        pltpu.SemaphoreType.DMA((34,)),
-        pltpu.SemaphoreType.DMA((34,)),
-        pltpu.SemaphoreType.DMA((9,)),
+        pltpu.SemaphoreType.DMA((56,)),
+        pltpu.SemaphoreType.DMA((56,)),
+        pltpu.SemaphoreType.DMA((11,)),
     ]
     extra = dict(collective_id=0, has_side_effects=True) if n_lon > 1 else {}
     results = pl.pallas_call(
         functools.partial(kernel_body, n_lon, n_sample, factor),
         out_shape=outs,
         in_specs=[vmem] * 4 + [far] * 9,
-        out_specs=(vmem,) * 6,
+        out_specs=(far, far) + (vmem,) * 4,
         scratch_shapes=scratch,
         compiler_params=pltpu.CompilerParams(vmem_limit_bytes=62 * 1024 * 1024, **extra),
     )(
@@ -657,7 +685,7 @@
         in_specs=[anywhere] * 6,
         out_specs=(anywhere,) * 6,
         scratch_shapes=[pltpu.VMEM(out.shape, out.dtype) for out in outs]
-        + [pltpu.SemaphoreType.DMA((2, 6))],
+        + [pltpu.SemaphoreType.DMA((2, 2 * CUTS + 4))],
     )(*results)
 
 

time: 43.4 us -> 46.4 us (1.069)
  Pallas kernels: 42.2 us -> 45 us
    pallas_call x1, Pallas kernels: 39.8 us -> 42.6 us  [block(): pl.pallas_call(functools.partial(kernel_body, n_lon, n_sample, factor), o...]
where the time goes in v7:
time: 46.4 us; the launch traced here: 45.6 us
  Pallas kernels  45 us (97%)
  between operations  0.64 us (1%)
    pallas_call x1, Pallas kernels, block(): pl.pallas_call(functools.partial(kernel_body, n_lon, n_sample, factor), o...  42.6 us
    pallas_call x1, Pallas kernels, block(): pl.pallas_call(deliver, out_shape=outs, in_specs=[anywhere] * 6, out_spec...  2.4 us

profile of v7, /device:TPU:0, one launch (start us, length us, event | category | flops | bytes accessed | tf_op | source)
XLA Modules:
  0.0 45.6 jit_solution(11758153786922748070)
XLA Ops:
  0.6 42.6 %shard_map.172 = (bf16[192,16,128]{2,1,0:T(8,128)(2,1)}, bf16[192,16,128]{2,1,0:T(8,128)(2,1)}, f32[12,768]{1,0:T(8,128)}, f32[12,768]{1,0:T(8,128)}, f32[7,7,12]{2,1,0:T(8,128)}, /*index=5*/f32[1,12]{1,0:T(1,128)}) custom-call(bf16[192,16,128]{2,1,0:T(8,128)(2,1)} %bitcast.10, s32[16,128]{1,0:T(8,128)} %sea_ref.1, f32[7,7,192]{2,1,0:T(8,128)} %bitcast.13, ...), custom_call_target="tpu_custom_call" | custom-call | tf_op jit(solution)/shard_map/pallas_call | solution.py:664
  43.2 2.4 %shard_map.173 = (bf16[192,16,128]{2,1,0:T(8,128)(2,1)}, bf16[192,16,128]{2,1,0:T(8,128)(2,1)}, f32[12,768]{1,0:T(8,128)}, f32[12,768]{1,0:T(8,128)}, f32[7,7,12]{2,1,0:T(8,128)}, /*index=5*/f32[1,12]{1,0:T(1,128)}) custom-call(bf16[192,16,128]{2,1,0:T(8,128)(2,1)} %get-tuple-element.18.refs_0_, bf16[192,16,128]{2,1,0:T(8,128)(2,1)} %get-tuple-element.19.refs_1_, ...), custom_call_target="tpu_custom_call" | custom-call | tf_op jit(solution)/shard_map/pallas_call | solution.py:682

commit v8 on v5

--- a/solution.py
+++ b/solution.py
@@ -170,6 +170,8 @@
     kparts,
     kslab,
     kout,
+    sout_buf,
+    gin_buf,
     send,
     recv,
     near,
@@ -380,26 +382,25 @@
 
     for at in range(HALO, LON + HALO, GROUP):
         field_spectrum(at, GROUP)
-    def filter_grads(parts, fresh):
+    def filter_grads(first, last):
         def one_tile(tile, carry):
             at = pl.multiple_of(tile * 8, 8)
             for half in range(0, SPEC, LAT):
-                lanes = slice(half, half + LAT)
+                totals = [None] * TAPS
+                for col in range(0, LON, 8):
+                    grads = gw[col : col + 8, pl.ds(at, 8), half : half + LAT]
+                    for a in range(TAPS):
+                        field = xh[col + a : col + a + 8, pl.ds(at, 8), half : half + LAT]
+                        part = jnp.sum(grads * field, axis=0)
+                        totals[a] = part if totals[a] is None else totals[a] + part
                 for a in range(TAPS):
-                    spot = slice(a * SPEC + half, a * SPEC + half + LAT)
-                    total = 0.0 if fresh else dkf[pl.ds(at, 8), spot]
-                    for col, count in parts:
-                        grads = gw[col : col + count, pl.ds(at, 8), lanes]
-                        field = xh[col + a : col + a + count, pl.ds(at, 8), lanes]
-                        total = total + jnp.sum(grads * field, axis=0)
-                    dkf[pl.ds(at, 8), spot] = total
+                    dkf[pl.ds(at, 8), a * SPEC + half : a * SPEC + half + LAT] = totals[a]
             return carry
 
-        lax.fori_loop(0, C // 8, one_tile, 0, unroll=2)
+        lax.fori_loop(first, last, one_tile, 0, unroll=2)
 
     in_groups(0, 2, forward_group)
     in_groups(0, 2, backward_mlp)
-    filter_grads([(GROUP, 2 * GROUP)], True)
     cells = slice(GROUP * LAT, 3 * GROUP * LAT)
     acc_out[...] = matmul_nt(cot_all[:, cells], hid_all[:, cells])
     acc_in[...] = matmul_nt(norm_all[:, cells], gp_all[:, cells])
@@ -466,11 +467,12 @@
             return to_slabs(kslab, 27)
 
         start(w_core())
-    filter_grads([(0, GROUP), (3 * GROUP, GROUP)], False)
+    filter_grads(0, C // 16)
     if remote:
         wait(w_core())
         wmid[...] = (wsend[core].astype(F32) + wcore[...].astype(F32)).astype(BF)
         start(w_own())
+    filter_grads(C // 16, C // 8)
 
     lanes = lax.broadcasted_iota(jnp.int32, (C, LAT), 1)
     total = jnp.where(lanes == TAPS * TAPS, jnp.sum(acc_gain[...], axis=1, keepdims=True), 0.0)
@@ -491,6 +493,12 @@
     if remote:
         start(k_core())
     in_groups(0, 4, finish_state)
+    sout_buf[...] = x32[...].reshape(C, LON, LAT).astype(BF)
+    leave = [
+        pltpu.make_async_copy(sout_buf, sout_ref, near.at[9]),
+        pltpu.make_async_copy(gin_buf, gin_ref, near.at[10]),
+    ]
+    leave[0].start()
     if remote:
         wait(k_core())
         kmid[...] = ksend[core] + kcore[...]
@@ -526,8 +534,8 @@
         g_left.wait()
     grad_spectrum(LON + HALO, HALO)
     backward_group(LON - GROUP)
-    sout_ref[...] = x32[...].reshape(C, LON, LAT).astype(BF)
-    gin_ref[...] = c32[...].reshape(C, LON, LAT).astype(BF)
+    gin_buf[...] = c32[...].reshape(C, LON, LAT).astype(BF)
+    leave[1].start()
     if remote:
         wait(w_all())
         weights = wslab[0].astype(F32)
@@ -552,6 +560,8 @@
     for a in range(TAPS):
         gk_ref[a] = small_t[a * TAPS : (a + 1) * TAPS, 0:OWN]
     gg_ref[...] = small_t[TAPS * TAPS : TAPS * TAPS + 1, 0:OWN]
+    for one in leave:
+        one.wait()
 
 
 def deliver(*refs):
@@ -628,16 +638,18 @@
         pltpu.VMEM((7, 8, LAT), F32),
         pltpu.VMEM((8, 8, LAT), F32),
         pltpu.VMEM((16, LAT), F32),
+        pltpu.VMEM((C, LON, LAT), BF),
+        pltpu.VMEM((C, LON, LAT), BF),
         pltpu.SemaphoreType.DMA((34,)),
         pltpu.SemaphoreType.DMA((34,)),
-        pltpu.SemaphoreType.DMA((9,)),
+        pltpu.SemaphoreType.DMA((11,)),
     ]
     extra = dict(collective_id=0, has_side_effects=True) if n_lon > 1 else {}
     results = pl.pallas_call(
         functools.partial(kernel_body, n_lon, n_sample, factor),
         out_shape=outs,
         in_specs=[vmem] * 4 + [far] * 9,
-        out_specs=(vmem,) * 6,
+        out_specs=(far, far) + (vmem,) * 4,
         scratch_shapes=scratch,
         compiler_params=pltpu.CompilerParams(vmem_limit_bytes=62 * 1024 * 1024, **extra),
     )(

time: 43.4 us -> 43 us (level)
  no operation moved by 1% of the time
where the time goes in v8:
time: 43 us; the launch traced here: 42.5 us
  Pallas kernels  41.8 us (97%)
  between operations  0.64 us (1%)
    pallas_call x1, Pallas kernels, block(): pl.pallas_call(functools.partial(kernel_body, n_lon, n_sample, factor), o...  39.4 us
    pallas_call x1, Pallas kernels, block(): pl.pallas_call(deliver, out_shape=outs, in_specs=[anywhere] * 6, out_spec...  2.4 us

profile of v8, /device:TPU:0, one launch (start us, length us, event | category | flops | bytes accessed | tf_op | source)
XLA Modules:
  0.0 42.5 jit_solution(17463668962446871943)
XLA Ops:
  0.6 39.4 %shard_map.172 = (bf16[192,16,128]{2,1,0:T(8,128)(2,1)}, bf16[192,16,128]{2,1,0:T(8,128)(2,1)}, f32[12,768]{1,0:T(8,128)}, f32[12,768]{1,0:T(8,128)}, f32[7,7,12]{2,1,0:T(8,128)}, /*index=5*/f32[1,12]{1,0:T(1,128)}) custom-call(bf16[192,16,128]{2,1,0:T(8,128)(2,1)} %bitcast.10, s32[16,128]{1,0:T(8,128)} %sea_ref.1, f32[7,7,192]{2,1,0:T(8,128)} %bitcast.13, ...), custom_call_target="tpu_custom_call" | custom-call | tf_op jit(solution)/shard_map/pallas_call | solution.py:648
  40.1 2.4 %shard_map.173 = (bf16[192,16,128]{2,1,0:T(8,128)(2,1)}, bf16[192,16,128]{2,1,0:T(8,128)(2,1)}, f32[12,768]{1,0:T(8,128)}, f32[12,768]{1,0:T(8,128)}, f32[7,7,12]{2,1,0:T(8,128)}, /*index=5*/f32[1,12]{1,0:T(1,128)}) custom-call(bf16[192,16,128]{2,1,0:T(8,128)(2,1)} %get-tuple-element.18.refs_0_, bf16[192,16,128]{2,1,0:T(8,128)(2,1)} %get-tuple-element.19.refs_1_, ...), custom_call_target="tpu_custom_call" | custom-call | tf_op jit(solution)/shard_map/pallas_call | solution.py:666

commit v9 on v8

--- a/solution.py
+++ b/solution.py
@@ -105,10 +105,10 @@
     n_lon,
     n_sample,
     factor,
-    state_ref,
     sea_ref,
     taps_ref,
     gain_ref,
+    state_far,
     cot_far,
     win_far,
     wout_far,
@@ -124,6 +124,7 @@
     gwout_ref,
     gk_ref,
     gg_ref,
+    state_ref,
     cot_ref,
     win_ref,
     wout_t,
@@ -192,8 +193,6 @@
             )
         )
     ]
-    for fetch in fetches:
-        fetch.start()
     remote = n_lon > 1
     if remote:
         lon = lax.axis_index("lon")
@@ -235,6 +234,11 @@
         ref[0:HALO] = ref[LON : LON + HALO]
         ref[LON + HALO : LON + 2 * HALO] = ref[HALO : 2 * HALO]
 
+    arrive = pltpu.make_async_copy(state_far, state_ref, near.at[11])
+    arrive.start()
+    for fetch in fetches:
+        fetch.start()
+    arrive.wait()
     x32[...] = state_ref[...].astype(F32).reshape(C * LON, LAT)
     for i in (0, 1, 2, 13, 14, 15):
         xa[HALO + i] = column(x32, i).astype(BF)
@@ -305,8 +309,12 @@
     def side_by_side(parts):
         return jnp.concatenate([parts[k] for k in range(GROUP)], axis=1)
 
+    def first_cell(col):
+        turned = col + LON - GROUP
+        return (turned % LON if isinstance(col, int) else lax.rem(turned, LON)) * LAT
+
     def lanes_of(col):
-        return pl.ds(pl.multiple_of(col * LAT, GROUP * LAT), GROUP * LAT)
+        return pl.ds(pl.multiple_of(first_cell(col), GROUP * LAT), GROUP * LAT)
 
     def forward_group(col):
         mixed = filtered(xh, col, False, back_f)
@@ -333,7 +341,7 @@
                 slope = gate + hidden * (1.0 - bent) * (
                     1.5957691216057308 + 0.8562577952712031 * square
                 )
-                at = pl.ds(pl.multiple_of(col * LAT + n, CELL_BLOCK), CELL_BLOCK)
+                at = pl.ds(pl.multiple_of(first_cell(col) + n, CELL_BLOCK), CELL_BLOCK)
                 hid_all[h : h + HID_BLOCK, at] = hidden.astype(BF)
                 gp_all[h : h + HID_BLOCK, at] = (grad_half * slope).astype(BF)
 
@@ -400,8 +408,7 @@
         lax.fori_loop(first, last, one_tile, 0, unroll=2)
 
     in_groups(0, 2, forward_group)
-    in_groups(0, 2, backward_mlp)
-    cells = slice(GROUP * LAT, 3 * GROUP * LAT)
+    cells = slice(0, LON * LAT // 2)
     acc_out[...] = matmul_nt(cot_all[:, cells], hid_all[:, cells])
     acc_in[...] = matmul_nt(norm_all[:, cells], gp_all[:, cells])
     if remote:
@@ -417,13 +424,10 @@
         x_right.wait()
     field_spectrum(0, HALO)
     forward_group(0)
-    backward_mlp(0)
-    if remote:
-        g_left.start()
-
-    for cells in (slice(0, GROUP * LAT), slice(3 * GROUP * LAT, LON * LAT)):
-        acc_out[...] += matmul_nt(cot_all[:, cells], hid_all[:, cells])
-        acc_in[...] += matmul_nt(norm_all[:, cells], gp_all[:, cells])
+
+    cells = slice(LON * LAT // 2, LON * LAT)
+    acc_out[...] += matmul_nt(cot_all[:, cells], hid_all[:, cells])
+    acc_in[...] += matmul_nt(norm_all[:, cells], gp_all[:, cells])
     wide = HID // 2
     for o in range(16):
         at = OWN * o
@@ -467,12 +471,16 @@
             return to_slabs(kslab, 27)
 
         start(w_core())
-    filter_grads(0, C // 16)
+    backward_mlp(0)
+    if remote:
+        g_left.start()
+    in_groups(0, 1, backward_mlp)
     if remote:
         wait(w_core())
         wmid[...] = (wsend[core].astype(F32) + wcore[...].astype(F32)).astype(BF)
         start(w_own())
-    filter_grads(C // 16, C // 8)
+    in_groups(1, 2, backward_mlp)
+    filter_grads(0, C // 8)
 
     lanes = lax.broadcasted_iota(jnp.int32, (C, LAT), 1)
     total = jnp.where(lanes == TAPS * TAPS, jnp.sum(acc_gain[...], axis=1, keepdims=True), 0.0)
@@ -492,17 +500,18 @@
         ksend[o % 2, o // 2] = dks[0, at : at + 8, :] + dks[1, at + 6 : at + 14, :]
     if remote:
         start(k_core())
-    in_groups(0, 4, finish_state)
+    in_groups(0, 2, finish_state)
+    if remote:
+        wait(k_core())
+        kmid[...] = ksend[core] + kcore[...]
+        start(k_own())
+    in_groups(2, 4, finish_state)
     sout_buf[...] = x32[...].reshape(C, LON, LAT).astype(BF)
     leave = [
         pltpu.make_async_copy(sout_buf, sout_ref, near.at[9]),
         pltpu.make_async_copy(gin_buf, gin_ref, near.at[10]),
     ]
     leave[0].start()
-    if remote:
-        wait(k_core())
-        kmid[...] = ksend[core] + kcore[...]
-        start(k_own())
 
     def backward_group(col):
         moved = filtered(gh, col, True, back_b)
@@ -511,13 +520,7 @@
             at = pl.ds(col + k, C, stride=LON)
             c32[at, :] = c32[at, :] * mask[k] + moved[k]
 
-    in_groups(0, 2, backward_group)
-    if remote:
-        g_right.wait()
-    else:
-        local_halo(ga)
-    grad_spectrum(0, HALO)
-    backward_group(0)
+    in_groups(0, 1, backward_group)
     if remote:
         wait(w_own())
         held = wmid[owner].astype(F32)
@@ -525,6 +528,14 @@
             held = held + wparts[d].astype(F32)
         wslab[lon] = held.astype(BF)
         start(w_all())
+    in_groups(1, 2, backward_group)
+    if remote:
+        g_right.wait()
+    else:
+        local_halo(ga)
+    grad_spectrum(0, HALO)
+    backward_group(0)
+    if remote:
         wait(k_own())
         held = kmid[owner]
         for d in range(len(owners)):
@@ -592,6 +603,7 @@
         shape((1, OWN), F32),
     )
     scratch = [
+        pltpu.VMEM((C, LON, LAT), BF),
         pltpu.VMEM((C, LON, LAT), BF),
         pltpu.VMEM((C, HID), BF),
         pltpu.VMEM((C, HID), BF),
@@ -642,21 +654,21 @@
         pltpu.VMEM((C, LON, LAT), BF),
         pltpu.SemaphoreType.DMA((34,)),
         pltpu.SemaphoreType.DMA((34,)),
-        pltpu.SemaphoreType.DMA((11,)),
+        pltpu.SemaphoreType.DMA((12,)),
     ]
     extra = dict(collective_id=0, has_side_effects=True) if n_lon > 1 else {}
     results = pl.pallas_call(
         functools.partial(kernel_body, n_lon, n_sample, factor),
         out_shape=outs,
-        in_specs=[vmem] * 4 + [far] * 9,
+        in_specs=[vmem] * 3 + [far] * 10,
         out_specs=(far, far) + (vmem,) * 4,
         scratch_shapes=scratch,
         compiler_params=pltpu.CompilerParams(vmem_limit_bytes=62 * 1024 * 1024, **extra),
     )(
-        state.reshape(C, LON, LAT),
         sea,
         taps.transpose(1, 2, 0),
         gain.reshape(1, C),
+        state.reshape(C, LON, LAT),
         cot.reshape(C, LON, LAT),
         win,
         wout.T,

time: 43 us -> 42.1 us (0.979)
  Pallas kernels: 41.8 us -> 40.9 us
    pallas_call x1, Pallas kernels: 39.4 us -> 38.5 us  [block(): pl.pallas_call(functools.partial(kernel_body, n_lon, n_sample, factor), o...]
where the time goes in v9:
time: 42.1 us; the launch traced here: 41.5 us
  Pallas kernels  40.9 us (97%)
  between operations  0.64 us (2%)
    pallas_call x1, Pallas kernels, block(): pl.pallas_call(functools.partial(kernel_body, n_lon, n_sample, factor), o...  38.5 us
    pallas_call x1, Pallas kernels, block(): pl.pallas_call(deliver, out_shape=outs, in_specs=[anywhere] * 6, out_spec...  2.4 us

profile of v9, /device:TPU:0, one launch (start us, length us, event | category | flops | bytes accessed | tf_op | source)
XLA Modules:
  0.0 41.5 jit_solution(538860985889058730)
XLA Ops:
  0.6 38.5 %shard_map.172 = (bf16[192,16,128]{2,1,0:T(8,128)(2,1)}, bf16[192,16,128]{2,1,0:T(8,128)(2,1)}, f32[12,768]{1,0:T(8,128)}, f32[12,768]{1,0:T(8,128)}, f32[7,7,12]{2,1,0:T(8,128)}, /*index=5*/f32[1,12]{1,0:T(1,128)}) custom-call(s32[16,128]{1,0:T(8,128)} %sea_ref.1, f32[7,7,192]{2,1,0:T(8,128)} %bitcast.13, f32[1,192]{1,0:T(1,128)} %bitcast.14, ...), custom_call_target="tpu_custom_call" | custom-call | tf_op jit(solution)/shard_map/pallas_call | solution.py:660
  39.1 2.4 %shard_map.173 = (bf16[192,16,128]{2,1,0:T(8,128)(2,1)}, bf16[192,16,128]{2,1,0:T(8,128)(2,1)}, f32[12,768]{1,0:T(8,128)}, f32[12,768]{1,0:T(8,128)}, f32[7,7,12]{2,1,0:T(8,128)}, /*index=5*/f32[1,12]{1,0:T(1,128)}) custom-call(bf16[192,16,128]{2,1,0:T(8,128)(2,1)} %get-tuple-element.18.refs_0_, bf16[192,16,128]{2,1,0:T(8,128)(2,1)} %get-tuple-element.19.refs_1_, ...), custom_call_target="tpu_custom_call" | custom-call | tf_op jit(solution)/shard_map/pallas_call | solution.py:678

commit v10 on v9

--- a/solution.py
+++ b/solution.py
@@ -203,12 +203,19 @@
         partner = {"sample": sample + 1 - 2 * core}
         right = {"lon": lax.rem(lon + 1, n_lon)}
         left = {"lon": lax.rem(lon + n_lon - 1, n_lon)}
-        owners = [lax.rem(owner + d, n_own) for d in range(1, n_own)]
-        slabs = [lax.rem(lon + d, n_lon) for d in range(1, n_lon)]
+        deep = n_own // 2
+        owners = [
+            lax.rem(owner // deep + far, 2) * deep + lax.rem(owner + step, deep)
+            for far, step in ((1, 2), (1, 1), (1, 3), (1, 0), (0, 2), (0, 1), (0, 3))
+        ]
+        slabs = [
+            2 * lax.rem(lon // 2 + step, n_lon // 2) + lax.rem(lon + side, 2)
+            for side, step in ((1, 2), (0, 2), (1, 1), (1, 3), (0, 1), (0, 3), (1, 0))
+        ]
         peers = (
-            [partner]
-            + [{"sample": 2 * other + core} for other in owners]
+            [{"sample": 2 * other + core} for other in owners]
             + [{"lon": other} for other in slabs]
+            + [partner]
         )
         barrier = pltpu.get_barrier_semaphore()
         for peer in peers:

time: 42.1 us -> 43.1 us (1.024)
  Pallas kernels: 40.9 us -> 42.3 us
    pallas_call x1, Pallas kernels: 38.5 us -> 39.9 us  [block(): pl.pallas_call(functools.partial(kernel_body, n_lon, n_sample, factor), o...]
where the time goes in v10:
time: 43.1 us; the launch traced here: 42.9 us
  Pallas kernels  42.3 us (98%)
  between operations  0.64 us (1%)
    pallas_call x1, Pallas kernels, block(): pl.pallas_call(functools.partial(kernel_body, n_lon, n_sample, factor), o...  39.9 us
    pallas_call x1, Pallas kernels, block(): pl.pallas_call(deliver, out_shape=outs, in_specs=[anywhere] * 6, out_spec...  2.4 us

profile of v10, /device:TPU:0, one launch (start us, length us, event | category | flops | bytes accessed | tf_op | source)
XLA Modules:
  0.0 42.9 jit_solution(15179735325909494520)
XLA Ops:
  0.6 39.9 %shard_map.172 = (bf16[192,16,128]{2,1,0:T(8,128)(2,1)}, bf16[192,16,128]{2,1,0:T(8,128)(2,1)}, f32[12,768]{1,0:T(8,128)}, f32[12,768]{1,0:T(8,128)}, f32[7,7,12]{2,1,0:T(8,128)}, /*index=5*/f32[1,12]{1,0:T(1,128)}) custom-call(s32[16,128]{1,0:T(8,128)} %sea_ref.1, f32[7,7,192]{2,1,0:T(8,128)} %bitcast.13, f32[1,192]{1,0:T(1,128)} %bitcast.14, ...), custom_call_target="tpu_custom_call" | custom-call | tf_op jit(solution)/shard_map/pallas_call | solution.py:667
  40.5 2.4 %shard_map.173 = (bf16[192,16,128]{2,1,0:T(8,128)(2,1)}, bf16[192,16,128]{2,1,0:T(8,128)(2,1)}, f32[12,768]{1,0:T(8,128)}, f32[12,768]{1,0:T(8,128)}, f32[7,7,12]{2,1,0:T(8,128)}, /*index=5*/f32[1,12]{1,0:T(1,128)}) custom-call(bf16[192,16,128]{2,1,0:T(8,128)(2,1)} %get-tuple-element.18.refs_0_, bf16[192,16,128]{2,1,0:T(8,128)(2,1)} %get-tuple-element.19.refs_1_, ...), custom_call_target="tpu_custom_call" | custom-call | tf_op jit(solution)/shard_map/pallas_call | solution.py:685

commit v11 on v9

--- a/solution.py
+++ b/solution.py
@@ -472,13 +472,12 @@
 
         start(w_core())
     backward_mlp(0)
-    if remote:
-        g_left.start()
     in_groups(0, 1, backward_mlp)
     if remote:
         wait(w_core())
         wmid[...] = (wsend[core].astype(F32) + wcore[...].astype(F32)).astype(BF)
         start(w_own())
+        g_left.start()
     in_groups(1, 2, backward_mlp)
     filter_grads(0, C // 8)
 

time: 42.1 us -> 42.6 us (1.012)
    pallas_call x1, Pallas kernels: 38.5 us -> 38.9 us  [block(): pl.pallas_call(functools.partial(kernel_body, n_lon, n_sample, factor), o...]
where the time goes in v11:
time: 42.6 us; the launch traced here: 41.9 us
  Pallas kernels  41.3 us (97%)
  between operations  0.64 us (2%)
    pallas_call x1, Pallas kernels, block(): pl.pallas_call(functools.partial(kernel_body, n_lon, n_sample, factor), o...  38.9 us
    pallas_call x1, Pallas kernels, block(): pl.pallas_call(deliver, out_shape=outs, in_specs=[anywhere] * 6, out_spec...  2.4 us

profile of v11, /device:TPU:0, one launch (start us, length us, event | category | flops | bytes accessed | tf_op | source)
XLA Modules:
  0.0 41.9 jit_solution(18192326204066835685)
XLA Ops:
  0.6 38.9 %shard_map.172 = (bf16[192,16,128]{2,1,0:T(8,128)(2,1)}, bf16[192,16,128]{2,1,0:T(8,128)(2,1)}, f32[12,768]{1,0:T(8,128)}, f32[12,768]{1,0:T(8,128)}, f32[7,7,12]{2,1,0:T(8,128)}, /*index=5*/f32[1,12]{1,0:T(1,128)}) custom-call(s32[16,128]{1,0:T(8,128)} %sea_ref.1, f32[7,7,192]{2,1,0:T(8,128)} %bitcast.13, f32[1,192]{1,0:T(1,128)} %bitcast.14, ...), custom_call_target="tpu_custom_call" | custom-call | tf_op jit(solution)/shard_map/pallas_call | solution.py:659
  39.5 2.4 %shard_map.173 = (bf16[192,16,128]{2,1,0:T(8,128)(2,1)}, bf16[192,16,128]{2,1,0:T(8,128)(2,1)}, f32[12,768]{1,0:T(8,128)}, f32[12,768]{1,0:T(8,128)}, f32[7,7,12]{2,1,0:T(8,128)}, /*index=5*/f32[1,12]{1,0:T(1,128)}) custom-call(bf16[192,16,128]{2,1,0:T(8,128)(2,1)} %get-tuple-element.18.refs_0_, bf16[192,16,128]{2,1,0:T(8,128)(2,1)} %get-tuple-element.19.refs_1_, ...), custom_call_target="tpu_custom_call" | custom-call | tf_op jit(solution)/shard_map/pallas_call | solution.py:677

commit v12 on v9

--- a/solution.py
+++ b/solution.py
@@ -279,7 +279,7 @@
         spectrum = matmul(doubled(ga[at : at + count]), field_g[:, SPEC:])
         gh[at : at + count] = spectrum.reshape(count, C, SPEC)
 
-    def filtered(field, col, flip, inverse):
+    def filtered(field, col, flip, inverse, exact):
         def one_tile(tile, carry):
             at = pl.multiple_of(tile * TILE, TILE)
             for half in range(0, SPEC, LAT):
@@ -293,15 +293,17 @@
                 total = tree_sum(terms)
                 high = total.astype(BF)
                 sum_high[:, pl.ds(at, TILE), half : half + LAT] = high
-                sum_low[:, pl.ds(at, TILE), half : half + LAT] = (
-                    total - high.astype(F32)
-                ).astype(BF)
+                if exact:
+                    low = (total - high.astype(F32)).astype(BF)
+                    sum_low[:, pl.ds(at, TILE), half : half + LAT] = low
             return carry
 
         lax.fori_loop(0, C // TILE, one_tile, 0, unroll=2)
         main = matmul(sum_high[...].reshape(GROUP * C, SPEC), inverse[...])
-        rest = matmul(sum_low[...].reshape(GROUP * C, SPEC), inverse[:, 0:LAT])
-        return (main[:, 0:LAT] + main[:, LAT:] + rest).reshape(GROUP, C, LAT)
+        both = main[:, 0:LAT] + main[:, LAT:]
+        if exact:
+            both = both + matmul(sum_low[...].reshape(GROUP * C, SPEC), inverse[:, 0:LAT])
+        return both.reshape(GROUP, C, LAT)
 
     def masks(col):
         return [sea_ref[pl.ds(col + k, 1), :].astype(F32) for k in range(GROUP)]
@@ -317,7 +319,7 @@
         return pl.ds(pl.multiple_of(first_cell(col), GROUP * LAT), GROUP * LAT)
 
     def forward_group(col):
-        mixed = filtered(xh, col, False, back_f)
+        mixed = filtered(xh, col, False, back_f, True)
         centred = mixed - jnp.mean(mixed, axis=1, keepdims=True)
         variance = jnp.mean(centred * centred, axis=1, keepdims=True)
         inv_scale = lax.rsqrt(variance + 1e-06)
@@ -514,7 +516,7 @@
     leave[0].start()
 
     def backward_group(col):
-        moved = filtered(gh, col, True, back_b)
+        moved = filtered(gh, col, True, back_b, False)
         mask = masks(col)
         for k in range(GROUP):
             at = pl.ds(col + k, C, stride=LON)

time: 42.1 us -> 42.1 us (level)
  no operation moved by 1% of the time
where the time goes in v12:
time: 42.1 us; the launch traced here: 41.5 us
  Pallas kernels  40.9 us (97%)
  between operations  0.64 us (2%)
    pallas_call x1, Pallas kernels, block(): pl.pallas_call(functools.partial(kernel_body, n_lon, n_sample, factor), o...  38.5 us
    pallas_call x1, Pallas kernels, block(): pl.pallas_call(deliver, out_shape=outs, in_specs=[anywhere] * 6, out_spec...  2.4 us

profile of v12, /device:TPU:0, one launch (start us, length us, event | category | flops | bytes accessed | tf_op | source)
XLA Modules:
  0.0 41.5 jit_solution(11937202722495254458)
XLA Ops:
  0.6 38.5 %shard_map.172 = (bf16[192,16,128]{2,1,0:T(8,128)(2,1)}, bf16[192,16,128]{2,1,0:T(8,128)(2,1)}, f32[12,768]{1,0:T(8,128)}, f32[12,768]{1,0:T(8,128)}, f32[7,7,12]{2,1,0:T(8,128)}, /*index=5*/f32[1,12]{1,0:T(1,128)}) custom-call(s32[16,128]{1,0:T(8,128)} %sea_ref.1, f32[7,7,192]{2,1,0:T(8,128)} %bitcast.13, f32[1,192]{1,0:T(1,128)} %bitcast.14, ...), custom_call_target="tpu_custom_call" | custom-call | tf_op jit(solution)/shard_map/pallas_call | solution.py:662
  39.1 2.4 %shard_map.173 = (bf16[192,16,128]{2,1,0:T(8,128)(2,1)}, bf16[192,16,128]{2,1,0:T(8,128)(2,1)}, f32[12,768]{1,0:T(8,128)}, f32[12,768]{1,0:T(8,128)}, f32[7,7,12]{2,1,0:T(8,128)}, /*index=5*/f32[1,12]{1,0:T(1,128)}) custom-call(bf16[192,16,128]{2,1,0:T(8,128)(2,1)} %get-tuple-element.18.refs_0_, bf16[192,16,128]{2,1,0:T(8,128)(2,1)} %get-tuple-element.19.refs_1_, ...), custom_call_target="tpu_custom_call" | custom-call | tf_op jit(solution)/shard_map/pallas_call | solution.py:680
